TPU v7x, 256 devices: a whole 4x4x8 slice. The times are simulated.
256 devices in a mesh: pair: 16 (over x, y), row: 16 (over z, core).
Axes of the slice: x: 4, y: 4, z: 8, core: 2. Of those that a mesh axis runs over, the one named last changes fastest.
Arguments:
- amplitudes: bfloat16 [768, 32, 9216], P(('pair', 'row')), may hold values from -6 to 6
- integrals: bfloat16 [16, 9216, 9216], P('pair', 'row'), may hold values from -0.015625 to 0.015625
- screen: int32 [768, 32], P(('pair', 'row')), may hold values 0 or 1
- live: int32 [32], replicated, may hold values 0 or 1
- owner: int32 [16], replicated, may hold values from 0 to 31, as said below
Outputs:
- ladder: bfloat16 [768, 9216], P(('pair', 'row'))
Inputs may be any that keep to these rules, and one draw needn't show every extreme that they name: `owner`: the 16 entries are distinct.
All inputs are finite; a program needn't handle non-finite values. No bound on the sum of `screen` on one device may be relied on, other than what follows from the above.
Results may differ from a plain program's by a relative error of at most 0.0012.
Values may be sent and summed in bfloat16 or wider, within the bound.
No kernel may reach another device: no remote copies, remote signals or barrier semaphores. Data moves between devices by JAX's collectives and lax.ppermute only.
A program may use at most 128 MiB of HBM per device.

v0:
```python
import functools
import math

import jax
import jax.numpy as jnp
from jax import lax
from jax.experimental import pallas as pl
from jax.experimental.pallas import tpu as pltpu
from jax.sharding import PartitionSpec as P

LANES = 128
CUT = 384
PARTS = 2
STEP = 2304

VMEM = pl.BlockSpec(memory_space=pltpu.VMEM)
SMEM = pl.BlockSpec(memory_space=pltpu.SMEM)
ANY = pl.BlockSpec(memory_space=pl.ANY)
SMALL = pl.CostEstimate(flops=1, bytes_accessed=1, transcendentals=0)


def pick_kernel(owner_hbm, amp_hbm, screen_hbm, live_hbm, out_ref, owner_ref, amp_ref, screen_ref, live_ref, packed, sems):
    slots = out_ref.shape[0]
    own, tiles, width = amp_ref.shape
    cuts = width // CUT
    small = [
        pltpu.make_async_copy(source, target, sems.at[i])
        for i, (source, target) in enumerate(
            ((owner_hbm, owner_ref), (screen_hbm, screen_ref), (live_hbm, live_ref))
        )
    ]
    large = [pltpu.make_async_copy(amp_hbm.at[r], amp_ref.at[r], sems.at[len(small) + r]) for r in range(own)]
    for copy in small + large:
        copy.start()
    for copy in small:
        copy.wait()
    slot = lax.broadcasted_iota(jnp.int32, (slots, tiles), 0)
    tile = lax.broadcasted_iota(jnp.int32, (slots, tiles), 1)
    wanted = jnp.zeros((slots, tiles), jnp.int32)
    for s in range(slots):
        wanted = jnp.where(slot == s, owner_ref[s], wanted)
    for r in range(own):
        kept = screen_ref[r : r + 1, :] * live_ref[...]
        chosen = jnp.where(wanted == tile, kept, 0).astype(jnp.float32).astype(jnp.bfloat16)
        large[r].wait()
        row = jnp.dot(chosen, amp_ref[r], preferred_element_type=jnp.float32)
        for q in range(cuts):
            for t in range(CUT // LANES):
                at = q * CUT + t * LANES
                packed[t, pl.ds(r * cuts + q, slots, stride=own * cuts), :] = row[:, at : at + LANES]
    for s in range(slots):
        for t in range(CUT // LANES):
            lines = packed[t, s * own * cuts : (s + 1) * own * cuts, :]
            out_ref[s, :, t * LANES : (t + 1) * LANES] = lines.astype(out_ref.dtype)


def pick(amplitudes, screen, live, owner):
    own, tiles, width = amplitudes.shape
    slots = owner.shape[0]
    lines = own * width // CUT
    return pl.pallas_call(
        pick_kernel,
        out_shape=jax.ShapeDtypeStruct((slots, lines, CUT), jnp.bfloat16),
        in_specs=[ANY] * 4,
        out_specs=VMEM,
        scratch_shapes=[
            pltpu.SMEM((slots,), jnp.int32),
            pltpu.VMEM(amplitudes.shape, amplitudes.dtype),
            pltpu.VMEM(screen.shape, jnp.int32),
            pltpu.VMEM((1, tiles), jnp.int32),
            pltpu.VMEM((CUT // LANES, slots * lines, LANES), jnp.float32),
            pltpu.SemaphoreType.DMA((3 + own,)),
        ],
        compiler_params=pltpu.CompilerParams(vmem_limit_bytes=16 << 20),
        name="pick",
    )(*[pltpu.with_memory_space_constraint(x, pltpu.HBM) for x in (owner, amplitudes, screen, live.reshape(1, tiles))])


def unpack_kernel(own, core_ref, in_ref, *refs):
    out_refs, packed = refs[:-1], refs[-1]
    group, lines, _ = in_ref.shape
    cuts = lines // own
    each = cuts // len(out_refs)
    side = math.isqrt(group)
    for s in range(group):
        to = jnp.where(core_ref[0] == 0, s, s % side * side + s // side)
        into = pl.ds(pl.multiple_of(to * lines, 8), lines)
        for t in range(CUT // LANES):
            packed[t, into, :] = in_ref[s, :, t * LANES : (t + 1) * LANES].astype(jnp.float32)
    for k, out_ref in enumerate(out_refs):
        for i in range(each):
            for t in range(CUT // LANES):
                rows = [packed[t, pl.ds(r * cuts + k * each + i, group, stride=lines), :] for r in range(own)]
                at = i * CUT + t * LANES
                out_ref[:, at : at + LANES] = jnp.concatenate(rows, axis=0).astype(out_ref.dtype)


def unpack(core, packed, own):
    group, lines, _ = packed.shape
    out = jax.ShapeDtypeStruct((own * group, lines // own * CUT // PARTS), packed.dtype)
    return pl.pallas_call(
        functools.partial(unpack_kernel, own),
        out_shape=[out] * PARTS,
        in_specs=[SMEM, VMEM],
        out_specs=[VMEM] * PARTS,
        scratch_shapes=[pltpu.VMEM((CUT // LANES, group * lines, LANES), jnp.float32)],
        compiler_params=pltpu.CompilerParams(vmem_limit_bytes=24 << 20),
        name="unpack",
    )(core, packed)


def stage_kernel(first, core_ref, mine_ref, theirs_ref, out_ref, token_ref, sems):
    columns, width = mine_ref.shape[0], out_ref.shape[1]
    at = pl.multiple_of(core_ref[0] * columns, columns)
    other = pl.multiple_of((1 - core_ref[0]) * columns, columns)
    part = pl.ds(first, width)
    one = pltpu.make_async_copy(mine_ref.at[:, part], out_ref.at[pl.ds(at, columns)], sems.at[0])
    two = pltpu.make_async_copy(theirs_ref.at[:, part], out_ref.at[pl.ds(other, columns)], sems.at[1])
    one.start()
    two.start()
    token_ref[...] = jnp.zeros_like(token_ref)
    one.wait()
    two.wait()


def stage(core, mine, theirs, k):
    columns, width = mine.shape
    each = width // PARTS
    return pl.pallas_call(
        functools.partial(stage_kernel, k * each),
        out_shape=[pltpu.VMEM((2 * columns, each), mine.dtype), jax.ShapeDtypeStruct((8, LANES), jnp.float32)],
        in_specs=[SMEM, ANY, ANY],
        out_specs=[VMEM, VMEM],
        scratch_shapes=[pltpu.SemaphoreType.DMA((2,))],
        compiler_params=pltpu.CompilerParams(vmem_limit_bytes=2 << 20),
        cost_estimate=SMALL,
        name=f"stage{k}",
    )(core, pltpu.with_memory_space_constraint(mine, pltpu.HBM), pltpu.with_memory_space_constraint(theirs, pltpu.HBM))


def product_kernel(plan, group, side, *refs):
    final = group is not None
    outs = side if final else 1
    operands = 1 + max(max(line) for line in plan)
    a_refs = refs[:operands]
    tile_ref = refs[operands]
    rest = refs[operands + 1 :]
    sorting = 1 if final else 0
    at_ref, rest = (rest[0], rest[1:]) if final else (None, rest)
    scratch = 2 + sorting
    carried = rest[: len(rest) - outs - scratch]
    out_refs = rest[len(carried) : len(carried) + outs]
    rows, total = rest[len(carried) + outs :][:2]
    at = pl.program_id(0)
    high = rows.shape[0] // len(plan)

    for step in range(len(plan[0])):

        @pl.when(at == step)
        def _(step=step):
            for o, line in enumerate(plan):
                rows[o * high : (o + 1) * high, :] = a_refs[line[step]][...]

    def add(columns):
        return lax.dot_general(
            rows[...], tile_ref[:, columns], (((1,), (1,)), ((), ())), preferred_element_type=jnp.float32
        )

    columns = pl.ds(pl.multiple_of(at * STEP, STEP), STEP)

    @pl.when(at == 0)
    def _():
        total[...] = carried[0][...] + add(columns) if carried else add(columns)

    @pl.when(at > 0)
    def _():
        total[...] += add(columns)

    @pl.when(at == pl.num_programs(0) - 1)
    def _():
        if not final:
            out_refs[0][...] = total[...]
            return
        ordered = rest[-1]
        pieces = total.shape[0] // group
        height = ordered.shape[0] // group
        used = pieces * total.shape[1] // LANES
        for q in range(group):
            if used < height:
                ordered[q * height + used : (q + 1) * height, :] = jnp.zeros((height - used, LANES), jnp.float32)
        for t in range(total.shape[1] // LANES):
            for j in range(pieces):
                ordered[pl.ds(t * pieces + j, group, stride=height), :] = total[
                    j * group : (j + 1) * group, t * LANES : (t + 1) * LANES
                ]
        block = ordered.shape[0] // side
        for d, out_ref in enumerate(out_refs):
            to = lax.rem(at_ref[0] + d, side)
            out_ref[...] = ordered[pl.ds(pl.multiple_of(to * block, block), block), :]


def padded(lines):
    return -(-lines // 8) * 8


def product(lines, tiles, carried=None, ends=None):
    operands, blocks, plan = [], [], []
    for line in lines:
        plan.append([])
        for step, (array, block) in enumerate(line):
            known = [i for i, other in enumerate(operands) if other is array]
            if known:
                blocks[known[0]][step] = block
            else:
                operands.append(array)
                blocks.append({step: block})
            plan[-1].append(known[0] if known else len(operands) - 1)
    high = operands[0].shape[0]
    steps = len(plan[0])
    columns = tiles.shape[0]
    rows = high * len(lines)

    def spec(used):
        low, top = min(used), max(used)
        base = used[low]
        return pl.BlockSpec((high, STEP), lambda s: (0, base + jnp.clip(s, low, top) - low))

    extra, specs = [], []
    group, side = None, None
    scratch = [pltpu.VMEM((rows, STEP), jnp.bfloat16), pltpu.VMEM((rows, columns), jnp.float32)]
    if ends is None:
        out, outs = (rows, columns), 1
    else:
        group, side, at = ends
        height = padded(rows // group * columns // LANES)
        out, outs = (group // side * height, LANES), side
        extra.append(at)
        specs.append(SMEM)
        scratch.append(pltpu.VMEM((group * height, LANES), jnp.float32))
    if carried is not None:
        extra.append(carried)
        specs.append(VMEM)
    made = pl.pallas_call(
        functools.partial(product_kernel, plan, group, side),
        grid=(steps,),
        out_shape=[jax.ShapeDtypeStruct(out, jnp.float32)] * outs,
        in_specs=[spec(used) for used in blocks] + [VMEM] + specs,
        out_specs=[pl.BlockSpec(out, lambda s: (0, 0))] * outs,
        scratch_shapes=scratch,
        compiler_params=pltpu.CompilerParams(vmem_limit_bytes=16 << 20),
        cost_estimate=SMALL,
        name=f"product{len(lines)}",
    )(*operands, tiles, *extra)
    return made[0] if ends is None else made


def middle_kernel(side, sizes, at_ref, *refs):
    in_refs, out_refs, totals = refs[: side * len(sizes)], refs[side * len(sizes) :][:side], refs[-len(sizes) :]
    for i, total in enumerate(totals):
        parts = in_refs[i * side : (i + 1) * side]
        summed = parts[0][...]
        for ref in parts[1:]:
            summed = summed + ref[...]
        total[...] = summed
    for d, out_ref in enumerate(out_refs):
        to = lax.rem(at_ref[0] + d, side)
        base = 0
        for size, total in zip(sizes, totals):
            out_ref[base : base + size, :] = total[pl.ds(pl.multiple_of(to * size, 8), size), :]
            base += size


def middle(at, *groups):
    side = len(groups[0])
    sizes = tuple(parts[0].shape[0] // side for parts in groups)
    flat = [part for parts in groups for part in parts]
    return pl.pallas_call(
        functools.partial(middle_kernel, side, sizes),
        out_shape=[jax.ShapeDtypeStruct((sum(sizes), LANES), jnp.float32)] * side,
        in_specs=[SMEM] + [VMEM] * len(flat),
        out_specs=[VMEM] * side,
        scratch_shapes=[pltpu.VMEM((size * side, LANES), jnp.float32) for size in sizes],
        compiler_params=pltpu.CompilerParams(vmem_limit_bytes=16 << 20),
        cost_estimate=SMALL,
        name="middle",
    )(at, *flat)


def total_kernel(own, side, groups, plan, *refs):
    in_refs, out_refs, total, blocks = refs[:side], refs[side:-2], refs[-2], refs[-1]
    summed = in_refs[0][...]
    for ref in in_refs[1:]:
        summed = summed + ref[...]
    total[...] = summed
    blocks[...] = jnp.zeros_like(blocks)
    base = 0
    for steps, tall in groups:
        pieces = own * len(steps)
        for o, step in enumerate(steps):
            for t in range(tall // pieces):
                at = base + t * pieces + o * own
                blocks[step, t * own : (t + 1) * own, :] = total[at : at + own, :]
        base += tall
    for out_ref, steps in zip(out_refs, plan):
        for i, step in enumerate(steps):
            out_ref[i] = blocks[step].astype(out_ref.dtype)


def totals(parts, own, groups, plan, columns):
    count = sum(len(steps) for steps, _ in groups)
    height = -(-own * columns // LANES // 16) * 16
    return pl.pallas_call(
        functools.partial(total_kernel, own, len(parts), groups, plan),
        out_shape=[jax.ShapeDtypeStruct((len(steps), height, LANES), jnp.bfloat16) for steps in plan],
        in_specs=[VMEM] * len(parts),
        out_specs=[VMEM] * len(plan),
        scratch_shapes=[pltpu.VMEM(parts[0].shape, jnp.float32), pltpu.VMEM((count, height, LANES), jnp.float32)],
        compiler_params=pltpu.CompilerParams(vmem_limit_bytes=16 << 20),
        cost_estimate=SMALL,
        name="totals",
    )(*parts)


def unique(blocks):
    arrays = []
    for array, _ in blocks:
        if not any(array is other for other in arrays):
            arrays.append(array)
    return arrays, [([i for i, other in enumerate(arrays) if other is array][0], at) for array, at in blocks]


def gather_kernel(plan, *refs):
    for i, (n, at) in enumerate(plan):
        refs[-1][i] = refs[n][at]


def gather(blocks):
    arrays, plan = unique(blocks)
    return pl.pallas_call(
        functools.partial(gather_kernel, plan),
        out_shape=jax.ShapeDtypeStruct((len(blocks),) + arrays[0].shape[1:], arrays[0].dtype),
        in_specs=[VMEM] * len(arrays),
        out_specs=VMEM,
        compiler_params=pltpu.CompilerParams(vmem_limit_bytes=16 << 20),
        cost_estimate=SMALL,
        name="gather",
    )(*arrays)


def place_kernel(plan, width, chip_ref, *refs):
    out_ref = refs[-1]
    own, count = out_ref.shape[0], len(plan)
    for step, (n, at) in enumerate(plan):
        source = lax.rem(chip_ref[0] - step + count, count)
        block = refs[n][at].astype(jnp.float32)
        row = [block[t * own : (t + 1) * own, :] for t in range(width // LANES)]
        into = pl.ds(pl.multiple_of(source * width, LANES), width)
        out_ref[:, into] = jnp.concatenate(row, axis=1).astype(out_ref.dtype)


def place(chip, blocks, own, width):
    arrays, plan = unique(blocks)
    return pl.pallas_call(
        functools.partial(place_kernel, plan, width),
        out_shape=jax.ShapeDtypeStruct((own, width * len(blocks)), jnp.bfloat16),
        in_specs=[SMEM] + [VMEM] * len(arrays),
        out_specs=VMEM,
        compiler_params=pltpu.CompilerParams(vmem_limit_bytes=16 << 20),
        cost_estimate=SMALL,
        name="place",
    )(chip, *arrays)


def after(x, *done):
    return lax.optimization_barrier((x,) + done)[0]


def local(amplitudes, integrals, screen, live, owner):
    own = amplitudes.shape[0]
    row_count = lax.axis_size("row")
    pairs = lax.axis_size("pair")
    chips = row_count // 2
    last = chips // 2
    row = lax.axis_index("row").astype(jnp.int32)
    core, chip = (row % 2).reshape(1), (row // 2).reshape(1)
    side = math.isqrt(pairs)
    pair = lax.axis_index("pair").astype(jnp.int32)
    slow = jnp.where(core == 0, pair // side, pair % side)
    fast = jnp.where(core == 0, pair % side, pair // side)

    def along(x, d):
        return lax.ppermute(x, "row", [(2 * z + c, 2 * ((z + d) % chips) + c) for z in range(chips) for c in range(2)])

    def shifted(x, d, slow):
        moves = []
        for p in range(pairs):
            over_x = p % side + (p // side + d) % side * side
            over_y = p // side * side + (p % side + d) % side
            for r in range(row_count):
                to = over_x if (r % 2 == 0) == slow else over_y
                moves.append((p * row_count + r, to * row_count + r))
        return lax.ppermute(x, ("pair", "row"), moves)

    mine = integrals[0]
    theirs = lax.ppermute(mine, "row", [(r, r ^ 1) for r in range(row_count)])
    columns = 2 * mine.shape[0]
    packed, core, chip, slow, fast = lax.optimization_barrier(
        (pick(amplitudes, screen, live, owner), core, chip, slow, fast)
    )
    start = unpack(core, lax.all_to_all(packed, "pair", split_axis=0, concat_axis=0, tiled=True), own)

    tiles, tokens = zip(*[stage(core, mine, theirs, k) for k in range(PARTS)])
    per = start[0].shape[1] // STEP
    half = per // 2 * STEP
    forward, backward = list(start), list(start)

    def whole(array):
        return [(array, b) for b in range(per)]

    def on(k, *done):
        forward[k] = along(after(forward[k], *done) if done else forward[k], 1)
        backward[k] = along(after(backward[k], *done) if done else backward[k], -1)

    def chain(k, lines, carried):
        ends = (pairs, side, slow) if k == PARTS - 1 else None
        return product(lines, tiles[k], carried, ends)

    def over_slow(parts):
        return [parts[0]] + [shifted(parts[d], d, True) for d in range(1, side)]

    def over_fast(parts):
        return [parts[0]] + [shifted(parts[d], d, False) for d in range(1, side)]

    near, made = [[whole(start[k])] for k in range(PARTS)], []
    for hop in range(1, last - 1):
        for k in range(PARTS):
            on(k, *([tokens[k]] if hop == last - 2 else []))
            near[k] += [whole(forward[k]), whole(backward[k])]
    for k in range(PARTS):
        made.append(chain(k, near[k], made[-1] if made else None))
    near_steps = (0,) + tuple(d % chips for hop in range(1, last - 1) for d in (-hop, hop))
    on(0)
    on(1, made[0])
    near_parts = over_slow(made[-1])
    far, ended = [], None
    for k in range(PARTS):
        low = along(after(forward[k][:, :half], made[-1][0]), 1)
        high = along(after(backward[k][:, half:], made[-1][0]), -1)
        far.append([whole(forward[k]), whole(backward[k]), [(low, 0), (high, 0)]])
    for k in range(PARTS):
        if k == PARTS - 1:
            ended = after(ended, *near_parts)
        ended = chain(k, far[k], ended)
    far_steps = ((1 - last) % chips, last - 1, last)
    groups = tuple((steps, padded(own * len(steps) * columns // LANES)) for steps in (near_steps, far_steps))
    plan = (far_steps[::-1], (0,), (1, 2), (chips - 1, chips - 2))
    parts = over_fast(middle(fast, near_parts, over_slow(ended)))
    distant, here, right, left = totals(parts, own, groups, plan, columns)
    distant, right, left = along(distant, last), along(right, 1), along(left, -1)
    right_two = along(gather([(right, 1), (distant, plan[0].index(last + 1))]), 1)
    left_two = along(gather([(left, 1), (distant, plan[0].index(last - 1))]), -1)
    blocks = {
        0: (here, 0),
        1: (right, 0),
        2: (right_two, 0),
        last - 1: (left_two, 1),
        last: (distant, plan[0].index(last)),
        last + 1: (right_two, 1),
        chips - 2: (left_two, 0),
        chips - 1: (left, 0),
    }
    return place(chip, [blocks[s] for s in range(chips)], own, columns)


def solution(mesh):
    return jax.shard_map(
        local,
        mesh=mesh,
        in_specs=(
            P(("pair", "row"), None, None),
            P("pair", "row", None),
            P(("pair", "row"), None),
            P(),
            P(),
        ),
        out_specs=P(("pair", "row"), None),
        check_vma=False,
    )
```

profile of v0, /device:TPU:6, one launch (start us, length us, event | category | flops | bytes accessed | tf_op | source)
XLA Modules:
  0.0 137.7 jit_solution(7515938092970839513)
XLA Ops:
  0.0 2.0 %pick.1 = bf16[16,72,384]{2,1,0:T(8,128)(2,1)S(1)} custom-call(s32[16]{0:T(128)} %owner_hbm.1, bf16[3,32,9216]{2,1,0:T(8,128)(2,1)} %amp_hbm.1, s32[3,32]{1,0:T(4,128)} %screen_hbm.1, s32[1,32]{1,0:T(1,128)} %bitcast.9), custom_call_target="tpu_custom_call" | custom-call | tf_op jit(solution)/shard_map/pick/pallas_call | solution.py:61
  2.0 21.1 %all_to_all.5.in_ref = bf16[16,72,384]{2,1,0:T(8,128)(2,1)S(1)} all-to-all(bf16[16,72,384]{2,1,0:T(8,128)(2,1)S(1)} %pick.1), channel_id=1, replica_groups=mesh['pair'=16,'row'=16] {'pair'}, dimensions={0} | all-to-all | bytes 1769472 | tf_op jit(solution)/shard_map/all_to_all | solution.py:410
  23.5 5.9 %collective-permute-start.6 = (bf16[48,4608]{1,0:T(8,128)(2,1)S(1)}, bf16[48,4608]{1,0:T(8,128)(2,1)S(1)}, u32[]{:S(2)}, u32[]{:S(2)}) collective-permute-start(bf16[48,4608]{1,0:T(8,128)(2,1)S(1)} %get-tuple-element.53.refs_0_), channel_id=1, source_target_pairs={{0,14},{1,15},{2,0},{3,1},{4,2},{5,3},{6,4},{7,5},{8,6},{9,7},{10,... | collective-permute-start | bytes 1327112 | tf_op jit(solution)/shard_map/ppermute | solution.py:392
  29.5 3.2 %collective-permute-start.1 = (bf16[48,4608]{1,0:T(8,128)(2,1)S(1)}, bf16[48,4608]{1,0:T(8,128)(2,1)S(1)}, u32[]{:S(2)}, u32[]{:S(2)}) collective-permute-start(bf16[48,4608]{1,0:T(8,128)(2,1)S(1)} %get-tuple-element.47.refs_0_), channel_id=1, source_target_pairs={{0,14},{1,15},{2,0},{3,1},{4,2},{5,3},{6,4},{7,5},{8,6},{9,7},{10,... | collective-permute-start | bytes 1327112 | tf_op jit(solution)/shard_map/ppermute | solution.py:392
  32.7 4.7 %stage0.1 = (bf16[1152,4608]{1,0:T(8,128)(2,1)S(1)}, f32[8,128]{1,0:T(8,128)}) custom-call(s32[1]{0:T(128)} %bitcast.1.core_ref, bf16[576,9216]{1,0:T(8,128)(2,1)} %bitcast.7, bf16[576,9216]{1,0:T(8,128)(2,1)} %collective-permute-done.2.theirs_ref), custom_call_target="tpu_custom_call" | custom-call | flops 1 | bytes 1 | tf_op jit(solution)/shard_map/stage0/pallas_call | solution.py:129
  37.4 2.7 %collective-permute-done.6.refs_2_ = bf16[48,4608]{1,0:T(8,128)(2,1)S(1)} collective-permute-done((bf16[48,4608]{1,0:T(8,128)(2,1)S(1)}, bf16[48,4608]{1,0:T(8,128)(2,1)S(1)}, u32[]{:S(2)}, u32[]{:S(2)}) %collective-permute-start.6) | collective-permute-done | bytes 442400 | tf_op jit(solution)/shard_map/ppermute | solution.py:392
  40.1 3.7 %collective-permute-start.8 = (bf16[48,4608]{1,0:T(8,128)(2,1)S(1)}, bf16[48,4608]{1,0:T(8,128)(2,1)S(1)}, u32[]{:S(2)}, u32[]{:S(2)}) collective-permute-start(bf16[48,4608]{1,0:T(8,128)(2,1)S(1)} %collective-permute-done.6.refs_2_), channel_id=1, source_target_pairs={{0,14},{1,15},{2,0},{3,1},{4,2},{5,3},{6,4},{7,5},{8,6},{9,7},{10,... | collective-permute-start | bytes 1327112 | tf_op jit(solution)/shard_map/ppermute | solution.py:392
  43.8 4.7 %stage1.1 = (bf16[1152,4608]{1,0:T(8,128)(2,1)S(1)}, f32[8,128]{1,0:T(8,128)}) custom-call(s32[1]{0:T(128)} %bitcast.1.core_ref, bf16[576,9216]{1,0:T(8,128)(2,1)} %bitcast.8, bf16[576,9216]{1,0:T(8,128)(2,1)} %collective-permute-done.2.theirs_ref), custom_call_target="tpu_custom_call" | custom-call | flops 1 | bytes 1 | tf_op jit(solution)/shard_map/stage1/pallas_call | solution.py:129
  49.6 3.7 %collective-permute-start.4 = (bf16[48,4608]{1,0:T(8,128)(2,1)S(1)}, bf16[48,4608]{1,0:T(8,128)(2,1)S(1)}, u32[]{:S(2)}, u32[]{:S(2)}) collective-permute-start(bf16[48,4608]{1,0:T(8,128)(2,1)S(1)} %collective-permute-done.1.refs_2_), channel_id=1, source_target_pairs={{0,14},{1,15},{2,0},{3,1},{4,2},{5,3},{6,4},{7,5},{8,6},{9,7},{10,... | collective-permute-start | bytes 1327112 | tf_op jit(solution)/shard_map/ppermute | solution.py:392
  53.3 5.8 %collective-permute-done.8.refs_4_ = bf16[48,4608]{1,0:T(8,128)(2,1)S(1)} collective-permute-done((bf16[48,4608]{1,0:T(8,128)(2,1)S(1)}, bf16[48,4608]{1,0:T(8,128)(2,1)S(1)}, u32[]{:S(2)}, u32[]{:S(2)}) %collective-permute-start.8) | collective-permute-done | bytes 442400 | tf_op jit(solution)/shard_map/ppermute | solution.py:392
  59.0 3.7 %collective-permute-start.17 = (bf16[48,4608]{1,0:T(8,128)(2,1)S(1)}, bf16[48,4608]{1,0:T(8,128)(2,1)S(1)}, u32[]{:S(2)}, u32[]{:S(2)}) collective-permute-start(bf16[48,4608]{1,0:T(8,128)(2,1)S(1)} %collective-permute-done.8.refs_4_), channel_id=1, source_target_pairs={{0,14},{1,15},{2,0},{3,1},{4,2},{5,3},{6,4},{7,5},{8,6},{9,7},{10,... | collective-permute-start | bytes 1327112 | tf_op jit(solution)/shard_map/ppermute | solution.py:392
  62.7 3.9 %product5.2.refs_7_ = f32[240,1152]{1,0:T(8,128)S(1)} custom-call(bf16[48,4608]{1,0:T(8,128)(2,1)S(1)} %get-tuple-element.53.refs_0_, bf16[48,4608]{1,0:T(8,128)(2,1)S(1)} %collective-permute-done.5.refs_1_, bf16[48,4608]{1,0:T(8,128)(2,1)S(1)} %collective-permute-done.6.refs_2_, bf16[48,4608]{1,0:T(8,128)(2,1)S(1)} %collective-permute-done.7.refs_3_, ...), custom_call_target="tpu_custom_call" | custom-call | flops 1 | bytes 1 | tf_op jit(solution)/shard_map/product5/pallas_call | solution.py:243
  66.6 1.9 %collective-permute-done.4.refs_4_ = bf16[48,4608]{1,0:T(8,128)(2,1)S(1)} collective-permute-done((bf16[48,4608]{1,0:T(8,128)(2,1)S(1)}, bf16[48,4608]{1,0:T(8,128)(2,1)S(1)}, u32[]{:S(2)}, u32[]{:S(2)}) %collective-permute-start.4) | collective-permute-done | bytes 442400 | tf_op jit(solution)/shard_map/ppermute | solution.py:392
  68.5 3.7 %collective-permute-start.13 = (bf16[48,4608]{1,0:T(8,128)(2,1)S(1)}, bf16[48,4608]{1,0:T(8,128)(2,1)S(1)}, u32[]{:S(2)}, u32[]{:S(2)}) collective-permute-start(bf16[48,4608]{1,0:T(8,128)(2,1)S(1)} %collective-permute-done.4.refs_4_), channel_id=1, source_target_pairs={{0,14},{1,15},{2,0},{3,1},{4,2},{5,3},{6,4},{7,5},{8,6},{9,7},{10,... | collective-permute-start | bytes 1327112 | tf_op jit(solution)/shard_map/ppermute | solution.py:392
  72.2 4.0 %product5.3 = (f32[544,128]{1,0:T(8,128)S(1)}, f32[544,128]{1,0:T(8,128)S(1)}, f32[544,128]{1,0:T(8,128)S(1)}, f32[544,128]{1,0:T(8,128)S(1)}) custom-call(bf16[48,4608]{1,0:T(8,128)(2,1)S(1)} %get-tuple-element.47.refs_0_, bf16[48,4608]{1,0:T(8,128)(2,1)S(1)} %collective-permute-done.refs_1_, bf16[48,4608]{1,0:T(8,128)(2,1)S(1)} %collective-permute-done.1.refs_2_, ...), custom_call_target="tpu_custom_call" | custom-call | flops 1 | bytes 1 | tf_op jit(solution)/shard_map/product5/pallas_call | solution.py:243
  76.3 1.7 %collective-permute-done.17.refs_1_ = bf16[48,4608]{1,0:T(8,128)(2,1)S(1)} collective-permute-done((bf16[48,4608]{1,0:T(8,128)(2,1)S(1)}, bf16[48,4608]{1,0:T(8,128)(2,1)S(1)}, u32[]{:S(2)}, u32[]{:S(2)}) %collective-permute-start.17) | collective-permute-done | bytes 442400 | tf_op jit(solution)/shard_map/ppermute | solution.py:392
  78.0 3.8 %collective-permute-start.19 = (bf16[48,2304]{1,0:T(8,128)(2,1)S(1)}, bf16[48,2304]{1,0:T(8,128)(2,1)S(1)}, u32[]{:S(2)}, u32[]{:S(2)}) collective-permute-start(bf16[48,2304]{1,0:T(8,128)(2,1)S(1)} %slice.19), channel_id=1, source_target_pairs={{0,14},{1,15},{2,0},{3,1},{4,2},{5,3},{6,4},{7,5},{8,6},{9,7},{10,... | collective-permute-start | bytes 663560 | tf_op jit(solution)/shard_map/ppermute | solution.py:392
  83.5 4.0 %collective-permute-done.13.refs_1_ = bf16[48,4608]{1,0:T(8,128)(2,1)S(1)} collective-permute-done((bf16[48,4608]{1,0:T(8,128)(2,1)S(1)}, bf16[48,4608]{1,0:T(8,128)(2,1)S(1)}, u32[]{:S(2)}, u32[]{:S(2)}) %collective-permute-start.13) | collective-permute-done | bytes 442400 | tf_op jit(solution)/shard_map/ppermute | solution.py:392
  88.1 3.0 %collective-permute-done.12.refs_0_ = bf16[48,4608]{1,0:T(8,128)(2,1)S(1)} collective-permute-done((bf16[48,4608]{1,0:T(8,128)(2,1)S(1)}, bf16[48,4608]{1,0:T(8,128)(2,1)S(1)}, u32[]{:S(2)}, u32[]{:S(2)}) %collective-permute-start.12) | collective-permute-done | bytes 442400 | tf_op jit(solution)/shard_map/ppermute | solution.py:392
  91.2 1.7 %collective-permute-start.9 = (f32[544,128]{1,0:T(8,128)S(1)}, f32[544,128]{1,0:T(8,128)S(1)}, u32[]{:S(2)}, u32[]{:S(2)}) collective-permute-start(f32[544,128]{1,0:T(8,128)S(1)} %get-tuple-element.59), channel_id=1, source_target_pairs={{0,64},{1,17},{2,66},{3,19},{4,68},{5,21},{6,70},{7,23},{8,72},{9,... | collective-permute-start | bytes 835592 | tf_op jit(solution)/shard_map/ppermute | solution.py:402
  95.1 3.9 %product3.2.refs_6_ = f32[144,1152]{1,0:T(8,128)S(1)} custom-call(bf16[48,4608]{1,0:T(8,128)(2,1)S(1)} %collective-permute-done.16.refs_0_, bf16[48,4608]{1,0:T(8,128)(2,1)S(1)} %collective-permute-done.17.refs_1_, bf16[48,2304]{1,0:T(8,128)(2,1)S(1)} %collective-permute-done.18.refs_2_, bf16[48,2304]{1,0:T(8,128)(2,1)S(1)} %collective-permute-done.19.refs_3_, ...), custom_call_target="tpu_custom_call" | custom-call | flops 1 | bytes 1 | tf_op jit(solution)/shard_map/product3/pallas_call | solution.py:243
  99.0 2.7 %collective-permute-done.14.refs_2_ = bf16[48,2304]{1,0:T(8,128)(2,1)S(1)} collective-permute-done((bf16[48,2304]{1,0:T(8,128)(2,1)S(1)}, bf16[48,2304]{1,0:T(8,128)(2,1)S(1)}, u32[]{:S(2)}, u32[]{:S(2)}) %collective-permute-start.14) | collective-permute-done | bytes 221216 | tf_op jit(solution)/shard_map/ppermute | solution.py:392
  101.7 4.1 %product3.3 = (f32[352,128]{1,0:T(8,128)S(1)}, f32[352,128]{1,0:T(8,128)S(1)}, f32[352,128]{1,0:T(8,128)S(1)}, f32[352,128]{1,0:T(8,128)S(1)}) custom-call(bf16[48,4608]{1,0:T(8,128)(2,1)S(1)} %collective-permute-done.12.refs_0_, bf16[48,4608]{1,0:T(8,128)(2,1)S(1)} %collective-permute-done.13.refs_1_, bf16[48,2304]{1,0:T(8,128)(2,1)S(1)} %collective-permute-done.14.refs_2_, ...), custom_call_target="tpu_custom_call" | custom-call | flops 1 | bytes 1 | tf_op jit(solution)/shard_map/product3/pallas_call | solution.py:243
  107.9 3.4 %collective-permute-done.20.refs_5_ = f32[352,128]{1,0:T(8,128)S(1)} collective-permute-done((f32[352,128]{1,0:T(8,128)S(1)}, f32[352,128]{1,0:T(8,128)S(1)}, u32[]{:S(2)}, u32[]{:S(2)}) %collective-permute-start.20) | collective-permute-done | bytes 180256 | tf_op jit(solution)/shard_map/ppermute | solution.py:402
  111.3 2.6 %collective-permute-done.21.refs_6_ = f32[352,128]{1,0:T(8,128)S(1)} collective-permute-done((f32[352,128]{1,0:T(8,128)S(1)}, f32[352,128]{1,0:T(8,128)S(1)}, u32[]{:S(2)}, u32[]{:S(2)}) %collective-permute-start.21) | collective-permute-done | bytes 180256 | tf_op jit(solution)/shard_map/ppermute | solution.py:402
  114.0 1.8 %collective-permute-done.22.refs_7_ = f32[352,128]{1,0:T(8,128)S(1)} collective-permute-done((f32[352,128]{1,0:T(8,128)S(1)}, f32[352,128]{1,0:T(8,128)S(1)}, u32[]{:S(2)}, u32[]{:S(2)}) %collective-permute-start.22) | collective-permute-done | bytes 180256 | tf_op jit(solution)/shard_map/ppermute | solution.py:402
  116.5 2.6 %collective-permute-start.24 = (f32[224,128]{1,0:T(8,128)S(1)}, f32[224,128]{1,0:T(8,128)S(1)}, u32[]{:S(2)}, u32[]{:S(2)}) collective-permute-start(f32[224,128]{1,0:T(8,128)S(1)} %get-tuple-element.75), channel_id=1, source_target_pairs={{0,32},{1,129},{2,34},{3,131},{4,36},{5,133},{6,38},{7,135},{8,40}... | collective-permute-start | bytes 344072 | tf_op jit(solution)/shard_map/ppermute | solution.py:402
  120.3 2.9 %collective-permute-done.23.refs_1_ = f32[224,128]{1,0:T(8,128)S(1)} collective-permute-done((f32[224,128]{1,0:T(8,128)S(1)}, f32[224,128]{1,0:T(8,128)S(1)}, u32[]{:S(2)}, u32[]{:S(2)}) %collective-permute-start.23) | collective-permute-done | bytes 114720 | tf_op jit(solution)/shard_map/ppermute | solution.py:402
  126.0 1.9 %collective-permute-start.26 = (bf16[2,32,128]{2,1,0:T(8,128)(2,1)S(1)}, bf16[2,32,128]{2,1,0:T(8,128)(2,1)S(1)}, u32[]{:S(2)}, u32[]{:S(2)}) collective-permute-start(bf16[2,32,128]{2,1,0:T(8,128)(2,1)S(1)} %get-tuple-element.78), channel_id=1, source_target_pairs={{0,2},{1,3},{2,4},{3,5},{4,6},{5,7},{6,8},{7,9},{8,10},{9,11},{10,... | collective-permute-start | bytes 49160 | tf_op jit(solution)/shard_map/ppermute | solution.py:392
  127.9 1.7 %collective-permute-done.29.refs_0_.refs_5_ = bf16[2,32,128]{2,1,0:T(8,128)(2,1)S(1)} collective-permute-done((bf16[2,32,128]{2,1,0:T(8,128)(2,1)S(1)}, bf16[2,32,128]{2,1,0:T(8,128)(2,1)S(1)}, u32[]{:S(2)}, u32[]{:S(2)}) %collective-permute-start.29) | collective-permute-done | bytes 16416 | tf_op jit(solution)/shard_map/ppermute | solution.py:392
  129.6 2.4 %collective-permute-done.27.refs_1_.refs_4_ = bf16[3,32,128]{2,1,0:T(8,128)(2,1)S(1)} collective-permute-done((bf16[3,32,128]{2,1,0:T(8,128)(2,1)S(1)}, bf16[3,32,128]{2,1,0:T(8,128)(2,1)S(1)}, u32[]{:S(2)}, u32[]{:S(2)}) %collective-permute-start.27) | collective-permute-done | bytes 24608 | tf_op jit(solution)/shard_map/ppermute | solution.py:392
  132.1 1.9 %collective-permute-start.28 = (bf16[2,32,128]{2,1,0:T(8,128)(2,1)S(1)}, bf16[2,32,128]{2,1,0:T(8,128)(2,1)S(1)}, u32[]{:S(2)}, u32[]{:S(2)}) collective-permute-start(bf16[2,32,128]{2,1,0:T(8,128)(2,1)S(1)} %gather.2), channel_id=1, source_target_pairs={{0,2},{1,3},{2,4},{3,5},{4,6},{5,7},{6,8},{7,9},{8,10},{9,11},{10,... | collective-permute-start | bytes 49160 | tf_op jit(solution)/shard_map/ppermute | solution.py:392
  (48 shorter events, 16.8 us)
Async XLA Ops:
  0.0 32.7 %collective-permute-start.2 = (bf16[576,9216]{1,0:T(8,128)(2,1)}, bf16[576,9216]{1,0:T(8,128)(2,1)}, u32[]{:S(2)}, u32[]{:S(2)}) collective-permute-start(bf16[576,9216]{1,0:T(8,128)(2,1)} %bitcast.6), channel_id=1, source_target_pairs={{0,1},{1,0},{2,3},{3,2},{4,5},{5,4},{6,7},{7,6},{8,9},{9,8},{10,11... | collective-permute-start | bytes 31850504 | tf_op jit(solution)/shard_map/ppermute | solution.py:405
  23.5 16.6 %collective-permute-start.6 = (bf16[48,4608]{1,0:T(8,128)(2,1)S(1)}, bf16[48,4608]{1,0:T(8,128)(2,1)S(1)}, u32[]{:S(2)}, u32[]{:S(2)}) collective-permute-start(bf16[48,4608]{1,0:T(8,128)(2,1)S(1)} %get-tuple-element.53.refs_0_), channel_id=1, source_target_pairs={{0,14},{1,15},{2,0},{3,1},{4,2},{5,3},{6,4},{7,5},{8,6},{9,7},{10,... | collective-permute-start | bytes 1327112 | tf_op jit(solution)/shard_map/ppermute | solution.py:392
  29.5 14.3 %collective-permute-start.5 = (bf16[48,4608]{1,0:T(8,128)(2,1)S(1)}, bf16[48,4608]{1,0:T(8,128)(2,1)S(1)}, u32[]{:S(2)}, u32[]{:S(2)}) collective-permute-start(bf16[48,4608]{1,0:T(8,128)(2,1)S(1)} %get-tuple-element.53.refs_0_), channel_id=1, source_target_pairs={{0,2},{1,3},{2,4},{3,5},{4,6},{5,7},{6,8},{7,9},{8,10},{9,11},{10,... | collective-permute-start | bytes 1327112 | tf_op jit(solution)/shard_map/ppermute | solution.py:392
  29.5 20.1 %collective-permute-start.1 = (bf16[48,4608]{1,0:T(8,128)(2,1)S(1)}, bf16[48,4608]{1,0:T(8,128)(2,1)S(1)}, u32[]{:S(2)}, u32[]{:S(2)}) collective-permute-start(bf16[48,4608]{1,0:T(8,128)(2,1)S(1)} %get-tuple-element.47.refs_0_), channel_id=1, source_target_pairs={{0,14},{1,15},{2,0},{3,1},{4,2},{5,3},{6,4},{7,5},{8,6},{9,7},{10,... | collective-permute-start | bytes 1327112 | tf_op jit(solution)/shard_map/ppermute | solution.py:392
  32.7 20.6 %collective-permute-start = (bf16[48,4608]{1,0:T(8,128)(2,1)S(1)}, bf16[48,4608]{1,0:T(8,128)(2,1)S(1)}, u32[]{:S(2)}, u32[]{:S(2)}) collective-permute-start(bf16[48,4608]{1,0:T(8,128)(2,1)S(1)} %get-tuple-element.47.refs_0_), channel_id=1, source_target_pairs={{0,2},{1,3},{2,4},{3,5},{4,6},{5,7},{6,8},{7,9},{8,10},{9,11},{10,... | collective-permute-start | bytes 1327112 | tf_op jit(solution)/shard_map/ppermute | solution.py:392
  40.1 19.0 %collective-permute-start.8 = (bf16[48,4608]{1,0:T(8,128)(2,1)S(1)}, bf16[48,4608]{1,0:T(8,128)(2,1)S(1)}, u32[]{:S(2)}, u32[]{:S(2)}) collective-permute-start(bf16[48,4608]{1,0:T(8,128)(2,1)S(1)} %collective-permute-done.6.refs_2_), channel_id=1, source_target_pairs={{0,14},{1,15},{2,0},{3,1},{4,2},{5,3},{6,4},{7,5},{8,6},{9,7},{10,... | collective-permute-start | bytes 1327112 | tf_op jit(solution)/shard_map/ppermute | solution.py:392
  43.8 19.0 %collective-permute-start.7 = (bf16[48,4608]{1,0:T(8,128)(2,1)S(1)}, bf16[48,4608]{1,0:T(8,128)(2,1)S(1)}, u32[]{:S(2)}, u32[]{:S(2)}) collective-permute-start(bf16[48,4608]{1,0:T(8,128)(2,1)S(1)} %collective-permute-done.5.refs_1_), channel_id=1, source_target_pairs={{0,2},{1,3},{2,4},{3,5},{4,6},{5,7},{6,8},{7,9},{8,10},{9,11},{10,... | collective-permute-start | bytes 1327112 | tf_op jit(solution)/shard_map/ppermute | solution.py:392
  49.6 19.0 %collective-permute-start.4 = (bf16[48,4608]{1,0:T(8,128)(2,1)S(1)}, bf16[48,4608]{1,0:T(8,128)(2,1)S(1)}, u32[]{:S(2)}, u32[]{:S(2)}) collective-permute-start(bf16[48,4608]{1,0:T(8,128)(2,1)S(1)} %collective-permute-done.1.refs_2_), channel_id=1, source_target_pairs={{0,14},{1,15},{2,0},{3,1},{4,2},{5,3},{6,4},{7,5},{8,6},{9,7},{10,... | collective-permute-start | bytes 1327112 | tf_op jit(solution)/shard_map/ppermute | solution.py:392
  53.3 19.0 %collective-permute-start.3 = (bf16[48,4608]{1,0:T(8,128)(2,1)S(1)}, bf16[48,4608]{1,0:T(8,128)(2,1)S(1)}, u32[]{:S(2)}, u32[]{:S(2)}) collective-permute-start(bf16[48,4608]{1,0:T(8,128)(2,1)S(1)} %collective-permute-done.refs_1_), channel_id=1, source_target_pairs={{0,2},{1,3},{2,4},{3,5},{4,6},{5,7},{6,8},{7,9},{8,10},{9,11},{10,... | collective-permute-start | bytes 1327112 | tf_op jit(solution)/shard_map/ppermute | solution.py:392
  59.0 19.0 %collective-permute-start.17 = (bf16[48,4608]{1,0:T(8,128)(2,1)S(1)}, bf16[48,4608]{1,0:T(8,128)(2,1)S(1)}, u32[]{:S(2)}, u32[]{:S(2)}) collective-permute-start(bf16[48,4608]{1,0:T(8,128)(2,1)S(1)} %collective-permute-done.8.refs_4_), channel_id=1, source_target_pairs={{0,14},{1,15},{2,0},{3,1},{4,2},{5,3},{6,4},{7,5},{8,6},{9,7},{10,... | collective-permute-start | bytes 1327112 | tf_op jit(solution)/shard_map/ppermute | solution.py:392
  62.7 19.1 %collective-permute-start.16 = (bf16[48,4608]{1,0:T(8,128)(2,1)S(1)}, bf16[48,4608]{1,0:T(8,128)(2,1)S(1)}, u32[]{:S(2)}, u32[]{:S(2)}) collective-permute-start(bf16[48,4608]{1,0:T(8,128)(2,1)S(1)} %collective-permute-done.7.refs_3_), channel_id=1, source_target_pairs={{0,2},{1,3},{2,4},{3,5},{4,6},{5,7},{6,8},{7,9},{8,10},{9,11},{10,... | collective-permute-start | bytes 1327112 | tf_op jit(solution)/shard_map/ppermute | solution.py:392
  68.5 19.0 %collective-permute-start.13 = (bf16[48,4608]{1,0:T(8,128)(2,1)S(1)}, bf16[48,4608]{1,0:T(8,128)(2,1)S(1)}, u32[]{:S(2)}, u32[]{:S(2)}) collective-permute-start(bf16[48,4608]{1,0:T(8,128)(2,1)S(1)} %collective-permute-done.4.refs_4_), channel_id=1, source_target_pairs={{0,14},{1,15},{2,0},{3,1},{4,2},{5,3},{6,4},{7,5},{8,6},{9,7},{10,... | collective-permute-start | bytes 1327112 | tf_op jit(solution)/shard_map/ppermute | solution.py:392
  72.2 19.0 %collective-permute-start.12 = (bf16[48,4608]{1,0:T(8,128)(2,1)S(1)}, bf16[48,4608]{1,0:T(8,128)(2,1)S(1)}, u32[]{:S(2)}, u32[]{:S(2)}) collective-permute-start(bf16[48,4608]{1,0:T(8,128)(2,1)S(1)} %collective-permute-done.3.refs_3_), channel_id=1, source_target_pairs={{0,2},{1,3},{2,4},{3,5},{4,6},{5,7},{6,8},{7,9},{8,10},{9,11},{10,... | collective-permute-start | bytes 1327112 | tf_op jit(solution)/shard_map/ppermute | solution.py:392
  78.0 14.9 %collective-permute-start.19 = (bf16[48,2304]{1,0:T(8,128)(2,1)S(1)}, bf16[48,2304]{1,0:T(8,128)(2,1)S(1)}, u32[]{:S(2)}, u32[]{:S(2)}) collective-permute-start(bf16[48,2304]{1,0:T(8,128)(2,1)S(1)} %slice.19), channel_id=1, source_target_pairs={{0,14},{1,15},{2,0},{3,1},{4,2},{5,3},{6,4},{7,5},{8,6},{9,7},{10,... | collective-permute-start | bytes 663560 | tf_op jit(solution)/shard_map/ppermute | solution.py:392
  81.8 12.7 %collective-permute-start.18 = (bf16[48,2304]{1,0:T(8,128)(2,1)S(1)}, bf16[48,2304]{1,0:T(8,128)(2,1)S(1)}, u32[]{:S(2)}, u32[]{:S(2)}) collective-permute-start(bf16[48,2304]{1,0:T(8,128)(2,1)S(1)} %slice.18), channel_id=1, source_target_pairs={{0,2},{1,3},{2,4},{3,5},{4,6},{5,7},{6,8},{7,9},{8,10},{9,11},{10,... | collective-permute-start | bytes 663560 | tf_op jit(solution)/shard_map/ppermute | solution.py:392
  81.9 17.1 %collective-permute-start.10 = (f32[544,128]{1,0:T(8,128)S(1)}, f32[544,128]{1,0:T(8,128)S(1)}, u32[]{:S(2)}, u32[]{:S(2)}) collective-permute-start(f32[544,128]{1,0:T(8,128)S(1)} %get-tuple-element.60), channel_id=1, source_target_pairs={{0,128},{1,33},{2,130},{3,35},{4,132},{5,37},{6,134},{7,39},{8,136... | collective-permute-start | bytes 835592 | tf_op jit(solution)/shard_map/ppermute | solution.py:402
  87.5 11.5 %collective-permute-start.11 = (f32[544,128]{1,0:T(8,128)S(1)}, f32[544,128]{1,0:T(8,128)S(1)}, u32[]{:S(2)}, u32[]{:S(2)}) collective-permute-start(f32[544,128]{1,0:T(8,128)S(1)} %get-tuple-element.61), channel_id=1, source_target_pairs={{0,192},{1,49},{2,194},{3,51},{4,196},{5,53},{6,198},{7,55},{8,200... | collective-permute-start | bytes 835592 | tf_op jit(solution)/shard_map/ppermute | solution.py:402
  91.2 7.8 %collective-permute-start.9 = (f32[544,128]{1,0:T(8,128)S(1)}, f32[544,128]{1,0:T(8,128)S(1)}, u32[]{:S(2)}, u32[]{:S(2)}) collective-permute-start(f32[544,128]{1,0:T(8,128)S(1)} %get-tuple-element.59), channel_id=1, source_target_pairs={{0,64},{1,17},{2,66},{3,19},{4,68},{5,21},{6,70},{7,23},{8,72},{9,... | collective-permute-start | bytes 835592 | tf_op jit(solution)/shard_map/ppermute | solution.py:402
  92.9 6.1 %collective-permute-start.15 = (bf16[48,2304]{1,0:T(8,128)(2,1)S(1)}, bf16[48,2304]{1,0:T(8,128)(2,1)S(1)}, u32[]{:S(2)}, u32[]{:S(2)}) collective-permute-start(bf16[48,2304]{1,0:T(8,128)(2,1)S(1)} %slice.17), channel_id=1, source_target_pairs={{0,14},{1,15},{2,0},{3,1},{4,2},{5,3},{6,4},{7,5},{8,6},{9,7},{10,... | collective-permute-start | bytes 663560 | tf_op jit(solution)/shard_map/ppermute | solution.py:392
  94.5 7.1 %collective-permute-start.14 = (bf16[48,2304]{1,0:T(8,128)(2,1)S(1)}, bf16[48,2304]{1,0:T(8,128)(2,1)S(1)}, u32[]{:S(2)}, u32[]{:S(2)}) collective-permute-start(bf16[48,2304]{1,0:T(8,128)(2,1)S(1)} %slice.16), channel_id=1, source_target_pairs={{0,2},{1,3},{2,4},{3,5},{4,6},{5,7},{6,8},{7,9},{8,10},{9,11},{10,... | collective-permute-start | bytes 663560 | tf_op jit(solution)/shard_map/ppermute | solution.py:392
  105.8 5.6 %collective-permute-start.20 = (f32[352,128]{1,0:T(8,128)S(1)}, f32[352,128]{1,0:T(8,128)S(1)}, u32[]{:S(2)}, u32[]{:S(2)}) collective-permute-start(f32[352,128]{1,0:T(8,128)S(1)} %get-tuple-element.70), channel_id=1, source_target_pairs={{0,64},{1,17},{2,66},{3,19},{4,68},{5,21},{6,70},{7,23},{8,72},{9,... | collective-permute-start | bytes 540680 | tf_op jit(solution)/shard_map/ppermute | solution.py:402
  106.8 7.1 %collective-permute-start.21 = (f32[352,128]{1,0:T(8,128)S(1)}, f32[352,128]{1,0:T(8,128)S(1)}, u32[]{:S(2)}, u32[]{:S(2)}) collective-permute-start(f32[352,128]{1,0:T(8,128)S(1)} %get-tuple-element.71), channel_id=1, source_target_pairs={{0,128},{1,33},{2,130},{3,35},{4,132},{5,37},{6,134},{7,39},{8,136... | collective-permute-start | bytes 540680 | tf_op jit(solution)/shard_map/ppermute | solution.py:402
  107.9 7.8 %collective-permute-start.22 = (f32[352,128]{1,0:T(8,128)S(1)}, f32[352,128]{1,0:T(8,128)S(1)}, u32[]{:S(2)}, u32[]{:S(2)}) collective-permute-start(f32[352,128]{1,0:T(8,128)S(1)} %get-tuple-element.72), channel_id=1, source_target_pairs={{0,192},{1,49},{2,194},{3,51},{4,196},{5,53},{6,198},{7,55},{8,200... | collective-permute-start | bytes 540680 | tf_op jit(solution)/shard_map/ppermute | solution.py:402
  115.9 7.3 %collective-permute-start.23 = (f32[224,128]{1,0:T(8,128)S(1)}, f32[224,128]{1,0:T(8,128)S(1)}, u32[]{:S(2)}, u32[]{:S(2)}) collective-permute-start(f32[224,128]{1,0:T(8,128)S(1)} %get-tuple-element.74), channel_id=1, source_target_pairs={{0,16},{1,65},{2,18},{3,67},{4,20},{5,69},{6,22},{7,71},{8,24},{9,... | collective-permute-start | bytes 344072 | tf_op jit(solution)/shard_map/ppermute | solution.py:402
  116.5 6.8 %collective-permute-start.24 = (f32[224,128]{1,0:T(8,128)S(1)}, f32[224,128]{1,0:T(8,128)S(1)}, u32[]{:S(2)}, u32[]{:S(2)}) collective-permute-start(f32[224,128]{1,0:T(8,128)S(1)} %get-tuple-element.75), channel_id=1, source_target_pairs={{0,32},{1,129},{2,34},{3,131},{4,36},{5,133},{6,38},{7,135},{8,40}... | collective-permute-start | bytes 344072 | tf_op jit(solution)/shard_map/ppermute | solution.py:402
  119.0 5.1 %collective-permute-start.25 = (f32[224,128]{1,0:T(8,128)S(1)}, f32[224,128]{1,0:T(8,128)S(1)}, u32[]{:S(2)}, u32[]{:S(2)}) collective-permute-start(f32[224,128]{1,0:T(8,128)S(1)} %get-tuple-element.76), channel_id=1, source_target_pairs={{0,48},{1,193},{2,50},{3,195},{4,52},{5,197},{6,54},{7,199},{8,56}... | collective-permute-start | bytes 344072 | tf_op jit(solution)/shard_map/ppermute | solution.py:402
  124.2 7.8 %collective-permute-start.27 = (bf16[3,32,128]{2,1,0:T(8,128)(2,1)S(1)}, bf16[3,32,128]{2,1,0:T(8,128)(2,1)S(1)}, u32[]{:S(2)}, u32[]{:S(2)}) collective-permute-start(bf16[3,32,128]{2,1,0:T(8,128)(2,1)S(1)} %get-tuple-element.79), channel_id=1, source_target_pairs={{0,8},{1,9},{2,10},{3,11},{4,12},{5,13},{6,14},{7,15},{8,0},{9,1},... | collective-permute-start | bytes 73736 | tf_op jit(solution)/shard_map/ppermute | solution.py:392
  125.9 3.7 %collective-permute-start.29 = (bf16[2,32,128]{2,1,0:T(8,128)(2,1)S(1)}, bf16[2,32,128]{2,1,0:T(8,128)(2,1)S(1)}, u32[]{:S(2)}, u32[]{:S(2)}) collective-permute-start(bf16[2,32,128]{2,1,0:T(8,128)(2,1)S(1)} %get-tuple-element.80), channel_id=1, source_target_pairs={{0,14},{1,15},{2,0},{3,1},{4,2},{5,3},{6,4},{7,5},{8,6},{9,7},{10,... | collective-permute-start | bytes 49160 | tf_op jit(solution)/shard_map/ppermute | solution.py:392
  126.0 6.1 %collective-permute-start.26 = (bf16[2,32,128]{2,1,0:T(8,128)(2,1)S(1)}, bf16[2,32,128]{2,1,0:T(8,128)(2,1)S(1)}, u32[]{:S(2)}, u32[]{:S(2)}) collective-permute-start(bf16[2,32,128]{2,1,0:T(8,128)(2,1)S(1)} %get-tuple-element.78), channel_id=1, source_target_pairs={{0,2},{1,3},{2,4},{3,5},{4,6},{5,7},{6,8},{7,9},{8,10},{9,11},{10,... | collective-permute-start | bytes 49160 | tf_op jit(solution)/shard_map/ppermute | solution.py:392
  132.0 3.7 %collective-permute-start.30 = (bf16[2,32,128]{2,1,0:T(8,128)(2,1)S(1)}, bf16[2,32,128]{2,1,0:T(8,128)(2,1)S(1)}, u32[]{:S(2)}, u32[]{:S(2)}) collective-permute-start(bf16[2,32,128]{2,1,0:T(8,128)(2,1)S(1)} %gather.3), channel_id=1, source_target_pairs={{0,14},{1,15},{2,0},{3,1},{4,2},{5,3},{6,4},{7,5},{8,6},{9,7},{10,... | collective-permute-start | bytes 49160 | tf_op jit(solution)/shard_map/ppermute | solution.py:392
  132.1 5.0 %collective-permute-start.28 = (bf16[2,32,128]{2,1,0:T(8,128)(2,1)S(1)}, bf16[2,32,128]{2,1,0:T(8,128)(2,1)S(1)}, u32[]{:S(2)}, u32[]{:S(2)}) collective-permute-start(bf16[2,32,128]{2,1,0:T(8,128)(2,1)S(1)} %gather.2), channel_id=1, source_target_pairs={{0,2},{1,3},{2,4},{3,5},{4,6},{5,7},{6,8},{7,9},{8,10},{9,11},{10,... | collective-permute-start | bytes 49160 | tf_op jit(solution)/shard_map/ppermute | solution.py:392
where the time goes:
time: 138 us
  starting transfers between devices  46.2 us (33%)
  waiting for transfers between devices  41.5 us (30%)
  Pallas kernels  28.6 us (21%)
  blocking collectives  21.1 us (15%)
    ppermute x21, starting transfers between devices, along(): lax.ppermute(x, 'row', [(2 * z + c, 2 * ((z + d) % chips) + c) for z in r...  35.7 us
    ppermute x21, waiting for transfers between devices, along(): lax.ppermute(x, 'row', [(2 * z + c, 2 * ((z + d) % chips) + c) for z in r...  29.9 us
    all_to_all x1, blocking collectives, local(): lax.all_to_all(packed, 'pair', split_axis=0, concat_axis=0, tiled=True)  21.1 us
    pallas_call x4, Pallas kernels, product(): pl.pallas_call(functools.partial(product_kernel, plan, group, side), grid...  15.9 us
    ppermute x9, waiting for transfers between devices, shifted(): return lax.ppermute(x, ('pair', 'row'), moves)  11.6 us
    ppermute x9, starting transfers between devices, shifted(): return lax.ppermute(x, ('pair', 'row'), moves)  10.6 us
    pallas_call x2, Pallas kernels, stage(): pl.pallas_call(functools.partial(stage_kernel, k * each), out_shape=[pltp...  9.4 us
  transfers between devices with their start and end apart: 31, of which 17 were waited for; matrix products, arithmetic and copies ran while one was open for 0% of the time, Pallas kernels for 17%

commit v1 on v0

--- a/solution.py
+++ b/solution.py
@@ -194,9 +194,13 @@
                     j * group : (j + 1) * group, t * LANES : (t + 1) * LANES
                 ]
         block = ordered.shape[0] // side
-        for d, out_ref in enumerate(out_refs):
+        for d, out_ref in zip(ways(side), out_refs):
             to = lax.rem(at_ref[0] + d, side)
             out_ref[...] = ordered[pl.ds(pl.multiple_of(to * block, block), block), :]
+
+
+def ways(side):
+    return [0] + sorted(range(1, side), key=lambda d: -min(d, side - d))
 
 
 def padded(lines):
@@ -262,7 +266,7 @@
         for ref in parts[1:]:
             summed = summed + ref[...]
         total[...] = summed
-    for d, out_ref in enumerate(out_refs):
+    for d, out_ref in zip(ways(side), out_refs):
         to = lax.rem(at_ref[0] + d, side)
         base = 0
         for size, total in zip(sizes, totals):
@@ -426,10 +430,10 @@
         return product(lines, tiles[k], carried, ends)
 
     def over_slow(parts):
-        return [parts[0]] + [shifted(parts[d], d, True) for d in range(1, side)]
+        return [parts[0]] + [shifted(part, d, True) for part, d in zip(parts[1:], ways(side)[1:])]
 
     def over_fast(parts):
-        return [parts[0]] + [shifted(parts[d], d, False) for d in range(1, side)]
+        return [parts[0]] + [shifted(part, d, False) for part, d in zip(parts[1:], ways(side)[1:])]
 
     near, made = [[whole(start[k])] for k in range(PARTS)], []
     for hop in range(1, last - 1):

time: 138 us -> 139 us (level)
  transfers between devices with their start and end apart: 31 -> 31, of which waited for: 17 -> 18; matrix products, arithmetic and copies ran while one was open for 0% -> 0% of each run, Pallas kernels for 17% -> 17%
where the time goes in v1:
time: 139 us
  starting transfers between devices  46.7 us (34%)
  waiting for transfers between devices  42.7 us (31%)
  Pallas kernels  28.6 us (21%)
  blocking collectives  21.1 us (15%)
    ppermute x21, starting transfers between devices, along(): lax.ppermute(x, 'row', [(2 * z + c, 2 * ((z + d) % chips) + c) for z in r...  35.2 us
    ppermute x21, waiting for transfers between devices, along(): lax.ppermute(x, 'row', [(2 * z + c, 2 * ((z + d) % chips) + c) for z in r...  30 us
    all_to_all x1, blocking collectives, local(): lax.all_to_all(packed, 'pair', split_axis=0, concat_axis=0, tiled=True)  21.1 us
    pallas_call x4, Pallas kernels, product(): pl.pallas_call(functools.partial(product_kernel, plan, group, side), grid...  15.9 us
    ppermute x9, waiting for transfers between devices, shifted(): return lax.ppermute(x, ('pair', 'row'), moves)  12.7 us
    ppermute x9, starting transfers between devices, shifted(): return lax.ppermute(x, ('pair', 'row'), moves)  11.5 us
    pallas_call x2, Pallas kernels, stage(): pl.pallas_call(functools.partial(stage_kernel, k * each), out_shape=[pltp...  9.4 us
  transfers between devices with their start and end apart: 31, of which 18 were waited for; matrix products, arithmetic and copies ran while one was open for 0% of the time, Pallas kernels for 17%

profile of v1, /device:TPU:6, one launch (start us, length us, event | category | flops | bytes accessed | tf_op | source)
XLA Modules:
  0.0 139.3 jit_solution(1912535637018296158)
XLA Ops:
  0.0 2.0 %pick.1 = bf16[16,72,384]{2,1,0:T(8,128)(2,1)S(1)} custom-call(s32[16]{0:T(128)} %owner_hbm.1, bf16[3,32,9216]{2,1,0:T(8,128)(2,1)} %amp_hbm.1, s32[3,32]{1,0:T(4,128)} %screen_hbm.1, s32[1,32]{1,0:T(1,128)} %bitcast.9), custom_call_target="tpu_custom_call" | custom-call | tf_op jit(solution)/shard_map/pick/pallas_call | solution.py:61
  2.0 21.1 %all_to_all.5.in_ref = bf16[16,72,384]{2,1,0:T(8,128)(2,1)S(1)} all-to-all(bf16[16,72,384]{2,1,0:T(8,128)(2,1)S(1)} %pick.1), channel_id=1, replica_groups=mesh['pair'=16,'row'=16] {'pair'}, dimensions={0} | all-to-all | bytes 1769472 | tf_op jit(solution)/shard_map/all_to_all | solution.py:414
  23.5 5.9 %collective-permute-start.6 = (bf16[48,4608]{1,0:T(8,128)(2,1)S(1)}, bf16[48,4608]{1,0:T(8,128)(2,1)S(1)}, u32[]{:S(2)}, u32[]{:S(2)}) collective-permute-start(bf16[48,4608]{1,0:T(8,128)(2,1)S(1)} %get-tuple-element.53.refs_0_), channel_id=1, source_target_pairs={{0,14},{1,15},{2,0},{3,1},{4,2},{5,3},{6,4},{7,5},{8,6},{9,7},{10,... | collective-permute-start | bytes 1327112 | tf_op jit(solution)/shard_map/ppermute | solution.py:396
  29.5 3.2 %collective-permute-start.1 = (bf16[48,4608]{1,0:T(8,128)(2,1)S(1)}, bf16[48,4608]{1,0:T(8,128)(2,1)S(1)}, u32[]{:S(2)}, u32[]{:S(2)}) collective-permute-start(bf16[48,4608]{1,0:T(8,128)(2,1)S(1)} %get-tuple-element.47.refs_0_), channel_id=1, source_target_pairs={{0,14},{1,15},{2,0},{3,1},{4,2},{5,3},{6,4},{7,5},{8,6},{9,7},{10,... | collective-permute-start | bytes 1327112 | tf_op jit(solution)/shard_map/ppermute | solution.py:396
  32.7 4.7 %stage0.1 = (bf16[1152,4608]{1,0:T(8,128)(2,1)S(1)}, f32[8,128]{1,0:T(8,128)}) custom-call(s32[1]{0:T(128)} %bitcast.1.core_ref, bf16[576,9216]{1,0:T(8,128)(2,1)} %bitcast.7, bf16[576,9216]{1,0:T(8,128)(2,1)} %collective-permute-done.2.theirs_ref), custom_call_target="tpu_custom_call" | custom-call | flops 1 | bytes 1 | tf_op jit(solution)/shard_map/stage0/pallas_call | solution.py:129
  37.4 2.7 %collective-permute-done.6.refs_2_ = bf16[48,4608]{1,0:T(8,128)(2,1)S(1)} collective-permute-done((bf16[48,4608]{1,0:T(8,128)(2,1)S(1)}, bf16[48,4608]{1,0:T(8,128)(2,1)S(1)}, u32[]{:S(2)}, u32[]{:S(2)}) %collective-permute-start.6) | collective-permute-done | bytes 442400 | tf_op jit(solution)/shard_map/ppermute | solution.py:396
  40.1 3.7 %collective-permute-start.8 = (bf16[48,4608]{1,0:T(8,128)(2,1)S(1)}, bf16[48,4608]{1,0:T(8,128)(2,1)S(1)}, u32[]{:S(2)}, u32[]{:S(2)}) collective-permute-start(bf16[48,4608]{1,0:T(8,128)(2,1)S(1)} %collective-permute-done.6.refs_2_), channel_id=1, source_target_pairs={{0,14},{1,15},{2,0},{3,1},{4,2},{5,3},{6,4},{7,5},{8,6},{9,7},{10,... | collective-permute-start | bytes 1327112 | tf_op jit(solution)/shard_map/ppermute | solution.py:396
  43.8 4.7 %stage1.1 = (bf16[1152,4608]{1,0:T(8,128)(2,1)S(1)}, f32[8,128]{1,0:T(8,128)}) custom-call(s32[1]{0:T(128)} %bitcast.1.core_ref, bf16[576,9216]{1,0:T(8,128)(2,1)} %bitcast.8, bf16[576,9216]{1,0:T(8,128)(2,1)} %collective-permute-done.2.theirs_ref), custom_call_target="tpu_custom_call" | custom-call | flops 1 | bytes 1 | tf_op jit(solution)/shard_map/stage1/pallas_call | solution.py:129
  49.6 3.7 %collective-permute-start.4 = (bf16[48,4608]{1,0:T(8,128)(2,1)S(1)}, bf16[48,4608]{1,0:T(8,128)(2,1)S(1)}, u32[]{:S(2)}, u32[]{:S(2)}) collective-permute-start(bf16[48,4608]{1,0:T(8,128)(2,1)S(1)} %collective-permute-done.1.refs_2_), channel_id=1, source_target_pairs={{0,14},{1,15},{2,0},{3,1},{4,2},{5,3},{6,4},{7,5},{8,6},{9,7},{10,... | collective-permute-start | bytes 1327112 | tf_op jit(solution)/shard_map/ppermute | solution.py:396
  53.3 5.8 %collective-permute-done.8.refs_4_ = bf16[48,4608]{1,0:T(8,128)(2,1)S(1)} collective-permute-done((bf16[48,4608]{1,0:T(8,128)(2,1)S(1)}, bf16[48,4608]{1,0:T(8,128)(2,1)S(1)}, u32[]{:S(2)}, u32[]{:S(2)}) %collective-permute-start.8) | collective-permute-done | bytes 442400 | tf_op jit(solution)/shard_map/ppermute | solution.py:396
  59.0 3.7 %collective-permute-start.17 = (bf16[48,4608]{1,0:T(8,128)(2,1)S(1)}, bf16[48,4608]{1,0:T(8,128)(2,1)S(1)}, u32[]{:S(2)}, u32[]{:S(2)}) collective-permute-start(bf16[48,4608]{1,0:T(8,128)(2,1)S(1)} %collective-permute-done.8.refs_4_), channel_id=1, source_target_pairs={{0,14},{1,15},{2,0},{3,1},{4,2},{5,3},{6,4},{7,5},{8,6},{9,7},{10,... | collective-permute-start | bytes 1327112 | tf_op jit(solution)/shard_map/ppermute | solution.py:396
  62.7 3.9 %product5.2.refs_7_ = f32[240,1152]{1,0:T(8,128)S(1)} custom-call(bf16[48,4608]{1,0:T(8,128)(2,1)S(1)} %get-tuple-element.53.refs_0_, bf16[48,4608]{1,0:T(8,128)(2,1)S(1)} %collective-permute-done.5.refs_1_, bf16[48,4608]{1,0:T(8,128)(2,1)S(1)} %collective-permute-done.6.refs_2_, bf16[48,4608]{1,0:T(8,128)(2,1)S(1)} %collective-permute-done.7.refs_3_, ...), custom_call_target="tpu_custom_call" | custom-call | flops 1 | bytes 1 | tf_op jit(solution)/shard_map/product5/pallas_call | solution.py:247
  66.6 1.9 %collective-permute-done.4.refs_4_ = bf16[48,4608]{1,0:T(8,128)(2,1)S(1)} collective-permute-done((bf16[48,4608]{1,0:T(8,128)(2,1)S(1)}, bf16[48,4608]{1,0:T(8,128)(2,1)S(1)}, u32[]{:S(2)}, u32[]{:S(2)}) %collective-permute-start.4) | collective-permute-done | bytes 442400 | tf_op jit(solution)/shard_map/ppermute | solution.py:396
  68.5 3.7 %collective-permute-start.13 = (bf16[48,4608]{1,0:T(8,128)(2,1)S(1)}, bf16[48,4608]{1,0:T(8,128)(2,1)S(1)}, u32[]{:S(2)}, u32[]{:S(2)}) collective-permute-start(bf16[48,4608]{1,0:T(8,128)(2,1)S(1)} %collective-permute-done.4.refs_4_), channel_id=1, source_target_pairs={{0,14},{1,15},{2,0},{3,1},{4,2},{5,3},{6,4},{7,5},{8,6},{9,7},{10,... | collective-permute-start | bytes 1327112 | tf_op jit(solution)/shard_map/ppermute | solution.py:396
  72.2 4.0 %product5.3 = (f32[544,128]{1,0:T(8,128)S(1)}, f32[544,128]{1,0:T(8,128)S(1)}, f32[544,128]{1,0:T(8,128)S(1)}, f32[544,128]{1,0:T(8,128)S(1)}) custom-call(bf16[48,4608]{1,0:T(8,128)(2,1)S(1)} %get-tuple-element.47.refs_0_, bf16[48,4608]{1,0:T(8,128)(2,1)S(1)} %collective-permute-done.refs_1_, bf16[48,4608]{1,0:T(8,128)(2,1)S(1)} %collective-permute-done.1.refs_2_, ...), custom_call_target="tpu_custom_call" | custom-call | flops 1 | bytes 1 | tf_op jit(solution)/shard_map/product5/pallas_call | solution.py:247
  76.3 1.7 %collective-permute-done.17.refs_1_ = bf16[48,4608]{1,0:T(8,128)(2,1)S(1)} collective-permute-done((bf16[48,4608]{1,0:T(8,128)(2,1)S(1)}, bf16[48,4608]{1,0:T(8,128)(2,1)S(1)}, u32[]{:S(2)}, u32[]{:S(2)}) %collective-permute-start.17) | collective-permute-done | bytes 442400 | tf_op jit(solution)/shard_map/ppermute | solution.py:396
  78.0 3.8 %collective-permute-start.19 = (bf16[48,2304]{1,0:T(8,128)(2,1)S(1)}, bf16[48,2304]{1,0:T(8,128)(2,1)S(1)}, u32[]{:S(2)}, u32[]{:S(2)}) collective-permute-start(bf16[48,2304]{1,0:T(8,128)(2,1)S(1)} %slice.19), channel_id=1, source_target_pairs={{0,14},{1,15},{2,0},{3,1},{4,2},{5,3},{6,4},{7,5},{8,6},{9,7},{10,... | collective-permute-start | bytes 663560 | tf_op jit(solution)/shard_map/ppermute | solution.py:396
  81.9 2.1 %collective-permute-start.10 = (f32[544,128]{1,0:T(8,128)S(1)}, f32[544,128]{1,0:T(8,128)S(1)}, u32[]{:S(2)}, u32[]{:S(2)}) collective-permute-start(f32[544,128]{1,0:T(8,128)S(1)} %get-tuple-element.60), channel_id=1, source_target_pairs={{0,64},{1,17},{2,66},{3,19},{4,68},{5,21},{6,70},{7,23},{8,72},{9,... | collective-permute-start | bytes 835592 | tf_op jit(solution)/shard_map/ppermute | solution.py:406
  84.0 3.5 %collective-permute-done.13.refs_1_ = bf16[48,4608]{1,0:T(8,128)(2,1)S(1)} collective-permute-done((bf16[48,4608]{1,0:T(8,128)(2,1)S(1)}, bf16[48,4608]{1,0:T(8,128)(2,1)S(1)}, u32[]{:S(2)}, u32[]{:S(2)}) %collective-permute-start.13) | collective-permute-done | bytes 442400 | tf_op jit(solution)/shard_map/ppermute | solution.py:396
  88.1 3.0 %collective-permute-done.12.refs_0_ = bf16[48,4608]{1,0:T(8,128)(2,1)S(1)} collective-permute-done((bf16[48,4608]{1,0:T(8,128)(2,1)S(1)}, bf16[48,4608]{1,0:T(8,128)(2,1)S(1)}, u32[]{:S(2)}, u32[]{:S(2)}) %collective-permute-start.12) | collective-permute-done | bytes 442400 | tf_op jit(solution)/shard_map/ppermute | solution.py:396
  92.6 2.2 %collective-permute-start.15 = (bf16[48,2304]{1,0:T(8,128)(2,1)S(1)}, bf16[48,2304]{1,0:T(8,128)(2,1)S(1)}, u32[]{:S(2)}, u32[]{:S(2)}) collective-permute-start(bf16[48,2304]{1,0:T(8,128)(2,1)S(1)} %slice.17), channel_id=1, source_target_pairs={{0,14},{1,15},{2,0},{3,1},{4,2},{5,3},{6,4},{7,5},{8,6},{9,7},{10,... | collective-permute-start | bytes 663560 | tf_op jit(solution)/shard_map/ppermute | solution.py:396
  94.8 3.9 %product3.2.refs_6_ = f32[144,1152]{1,0:T(8,128)S(1)} custom-call(bf16[48,4608]{1,0:T(8,128)(2,1)S(1)} %collective-permute-done.16.refs_0_, bf16[48,4608]{1,0:T(8,128)(2,1)S(1)} %collective-permute-done.17.refs_1_, bf16[48,2304]{1,0:T(8,128)(2,1)S(1)} %collective-permute-done.18.refs_2_, bf16[48,2304]{1,0:T(8,128)(2,1)S(1)} %collective-permute-done.19.refs_3_, ...), custom_call_target="tpu_custom_call" | custom-call | flops 1 | bytes 1 | tf_op jit(solution)/shard_map/product3/pallas_call | solution.py:247
  99.2 2.7 %collective-permute-done.14.refs_2_ = bf16[48,2304]{1,0:T(8,128)(2,1)S(1)} collective-permute-done((bf16[48,2304]{1,0:T(8,128)(2,1)S(1)}, bf16[48,2304]{1,0:T(8,128)(2,1)S(1)}, u32[]{:S(2)}, u32[]{:S(2)}) %collective-permute-start.14) | collective-permute-done | bytes 221216 | tf_op jit(solution)/shard_map/ppermute | solution.py:396
  101.9 4.1 %product3.3 = (f32[352,128]{1,0:T(8,128)S(1)}, f32[352,128]{1,0:T(8,128)S(1)}, f32[352,128]{1,0:T(8,128)S(1)}, f32[352,128]{1,0:T(8,128)S(1)}) custom-call(bf16[48,4608]{1,0:T(8,128)(2,1)S(1)} %collective-permute-done.12.refs_0_, bf16[48,4608]{1,0:T(8,128)(2,1)S(1)} %collective-permute-done.13.refs_1_, bf16[48,2304]{1,0:T(8,128)(2,1)S(1)} %collective-permute-done.14.refs_2_, ...), custom_call_target="tpu_custom_call" | custom-call | flops 1 | bytes 1 | tf_op jit(solution)/shard_map/product3/pallas_call | solution.py:247
  106.8 2.6 %collective-permute-start.21 = (f32[352,128]{1,0:T(8,128)S(1)}, f32[352,128]{1,0:T(8,128)S(1)}, u32[]{:S(2)}, u32[]{:S(2)}) collective-permute-start(f32[352,128]{1,0:T(8,128)S(1)} %get-tuple-element.71), channel_id=1, source_target_pairs={{0,64},{1,17},{2,66},{3,19},{4,68},{5,21},{6,70},{7,23},{8,72},{9,... | collective-permute-start | bytes 540680 | tf_op jit(solution)/shard_map/ppermute | solution.py:406
  109.4 3.7 %collective-permute-done.20.refs_5_ = f32[352,128]{1,0:T(8,128)S(1)} collective-permute-done((f32[352,128]{1,0:T(8,128)S(1)}, f32[352,128]{1,0:T(8,128)S(1)}, u32[]{:S(2)}, u32[]{:S(2)}) %collective-permute-start.20) | collective-permute-done | bytes 180256 | tf_op jit(solution)/shard_map/ppermute | solution.py:406
  113.7 4.3 %collective-permute-done.22.refs_7_ = f32[352,128]{1,0:T(8,128)S(1)} collective-permute-done((f32[352,128]{1,0:T(8,128)S(1)}, f32[352,128]{1,0:T(8,128)S(1)}, u32[]{:S(2)}, u32[]{:S(2)}) %collective-permute-start.22) | collective-permute-done | bytes 180256 | tf_op jit(solution)/shard_map/ppermute | solution.py:406
  119.1 3.0 %collective-permute-start.25 = (f32[224,128]{1,0:T(8,128)S(1)}, f32[224,128]{1,0:T(8,128)S(1)}, u32[]{:S(2)}, u32[]{:S(2)}) collective-permute-start(f32[224,128]{1,0:T(8,128)S(1)} %get-tuple-element.76), channel_id=1, source_target_pairs={{0,48},{1,193},{2,50},{3,195},{4,52},{5,197},{6,54},{7,199},{8,56}... | collective-permute-start | bytes 344072 | tf_op jit(solution)/shard_map/ppermute | solution.py:406
  122.1 2.5 %collective-permute-done.23.refs_1_ = f32[224,128]{1,0:T(8,128)S(1)} collective-permute-done((f32[224,128]{1,0:T(8,128)S(1)}, f32[224,128]{1,0:T(8,128)S(1)}, u32[]{:S(2)}, u32[]{:S(2)}) %collective-permute-start.23) | collective-permute-done | bytes 114720 | tf_op jit(solution)/shard_map/ppermute | solution.py:406
  127.0 2.0 %collective-permute-start.26 = (bf16[2,32,128]{2,1,0:T(8,128)(2,1)S(1)}, bf16[2,32,128]{2,1,0:T(8,128)(2,1)S(1)}, u32[]{:S(2)}, u32[]{:S(2)}) collective-permute-start(bf16[2,32,128]{2,1,0:T(8,128)(2,1)S(1)} %get-tuple-element.78), channel_id=1, source_target_pairs={{0,2},{1,3},{2,4},{3,5},{4,6},{5,7},{6,8},{7,9},{8,10},{9,11},{10,... | collective-permute-start | bytes 49160 | tf_op jit(solution)/shard_map/ppermute | solution.py:396
  130.7 2.9 %collective-permute-done.27.refs_1_.refs_4_ = bf16[3,32,128]{2,1,0:T(8,128)(2,1)S(1)} collective-permute-done((bf16[3,32,128]{2,1,0:T(8,128)(2,1)S(1)}, bf16[3,32,128]{2,1,0:T(8,128)(2,1)S(1)}, u32[]{:S(2)}, u32[]{:S(2)}) %collective-permute-start.27) | collective-permute-done | bytes 24608 | tf_op jit(solution)/shard_map/ppermute | solution.py:396
  133.6 2.0 %collective-permute-start.28 = (bf16[2,32,128]{2,1,0:T(8,128)(2,1)S(1)}, bf16[2,32,128]{2,1,0:T(8,128)(2,1)S(1)}, u32[]{:S(2)}, u32[]{:S(2)}) collective-permute-start(bf16[2,32,128]{2,1,0:T(8,128)(2,1)S(1)} %gather.2), channel_id=1, source_target_pairs={{0,2},{1,3},{2,4},{3,5},{4,6},{5,7},{6,8},{7,9},{8,10},{9,11},{10,... | collective-permute-start | bytes 49160 | tf_op jit(solution)/shard_map/ppermute | solution.py:396
  (48 shorter events, 14.6 us)
Async XLA Ops:
  0.0 32.7 %collective-permute-start.2 = (bf16[576,9216]{1,0:T(8,128)(2,1)}, bf16[576,9216]{1,0:T(8,128)(2,1)}, u32[]{:S(2)}, u32[]{:S(2)}) collective-permute-start(bf16[576,9216]{1,0:T(8,128)(2,1)} %bitcast.6), channel_id=1, source_target_pairs={{0,1},{1,0},{2,3},{3,2},{4,5},{5,4},{6,7},{7,6},{8,9},{9,8},{10,11... | collective-permute-start | bytes 31850504 | tf_op jit(solution)/shard_map/ppermute | solution.py:409
  23.5 16.6 %collective-permute-start.6 = (bf16[48,4608]{1,0:T(8,128)(2,1)S(1)}, bf16[48,4608]{1,0:T(8,128)(2,1)S(1)}, u32[]{:S(2)}, u32[]{:S(2)}) collective-permute-start(bf16[48,4608]{1,0:T(8,128)(2,1)S(1)} %get-tuple-element.53.refs_0_), channel_id=1, source_target_pairs={{0,14},{1,15},{2,0},{3,1},{4,2},{5,3},{6,4},{7,5},{8,6},{9,7},{10,... | collective-permute-start | bytes 1327112 | tf_op jit(solution)/shard_map/ppermute | solution.py:396
  29.5 14.3 %collective-permute-start.5 = (bf16[48,4608]{1,0:T(8,128)(2,1)S(1)}, bf16[48,4608]{1,0:T(8,128)(2,1)S(1)}, u32[]{:S(2)}, u32[]{:S(2)}) collective-permute-start(bf16[48,4608]{1,0:T(8,128)(2,1)S(1)} %get-tuple-element.53.refs_0_), channel_id=1, source_target_pairs={{0,2},{1,3},{2,4},{3,5},{4,6},{5,7},{6,8},{7,9},{8,10},{9,11},{10,... | collective-permute-start | bytes 1327112 | tf_op jit(solution)/shard_map/ppermute | solution.py:396
  29.5 20.1 %collective-permute-start.1 = (bf16[48,4608]{1,0:T(8,128)(2,1)S(1)}, bf16[48,4608]{1,0:T(8,128)(2,1)S(1)}, u32[]{:S(2)}, u32[]{:S(2)}) collective-permute-start(bf16[48,4608]{1,0:T(8,128)(2,1)S(1)} %get-tuple-element.47.refs_0_), channel_id=1, source_target_pairs={{0,14},{1,15},{2,0},{3,1},{4,2},{5,3},{6,4},{7,5},{8,6},{9,7},{10,... | collective-permute-start | bytes 1327112 | tf_op jit(solution)/shard_map/ppermute | solution.py:396
  32.7 20.6 %collective-permute-start = (bf16[48,4608]{1,0:T(8,128)(2,1)S(1)}, bf16[48,4608]{1,0:T(8,128)(2,1)S(1)}, u32[]{:S(2)}, u32[]{:S(2)}) collective-permute-start(bf16[48,4608]{1,0:T(8,128)(2,1)S(1)} %get-tuple-element.47.refs_0_), channel_id=1, source_target_pairs={{0,2},{1,3},{2,4},{3,5},{4,6},{5,7},{6,8},{7,9},{8,10},{9,11},{10,... | collective-permute-start | bytes 1327112 | tf_op jit(solution)/shard_map/ppermute | solution.py:396
  40.1 19.0 %collective-permute-start.8 = (bf16[48,4608]{1,0:T(8,128)(2,1)S(1)}, bf16[48,4608]{1,0:T(8,128)(2,1)S(1)}, u32[]{:S(2)}, u32[]{:S(2)}) collective-permute-start(bf16[48,4608]{1,0:T(8,128)(2,1)S(1)} %collective-permute-done.6.refs_2_), channel_id=1, source_target_pairs={{0,14},{1,15},{2,0},{3,1},{4,2},{5,3},{6,4},{7,5},{8,6},{9,7},{10,... | collective-permute-start | bytes 1327112 | tf_op jit(solution)/shard_map/ppermute | solution.py:396
  43.8 19.0 %collective-permute-start.7 = (bf16[48,4608]{1,0:T(8,128)(2,1)S(1)}, bf16[48,4608]{1,0:T(8,128)(2,1)S(1)}, u32[]{:S(2)}, u32[]{:S(2)}) collective-permute-start(bf16[48,4608]{1,0:T(8,128)(2,1)S(1)} %collective-permute-done.5.refs_1_), channel_id=1, source_target_pairs={{0,2},{1,3},{2,4},{3,5},{4,6},{5,7},{6,8},{7,9},{8,10},{9,11},{10,... | collective-permute-start | bytes 1327112 | tf_op jit(solution)/shard_map/ppermute | solution.py:396
  49.6 19.0 %collective-permute-start.4 = (bf16[48,4608]{1,0:T(8,128)(2,1)S(1)}, bf16[48,4608]{1,0:T(8,128)(2,1)S(1)}, u32[]{:S(2)}, u32[]{:S(2)}) collective-permute-start(bf16[48,4608]{1,0:T(8,128)(2,1)S(1)} %collective-permute-done.1.refs_2_), channel_id=1, source_target_pairs={{0,14},{1,15},{2,0},{3,1},{4,2},{5,3},{6,4},{7,5},{8,6},{9,7},{10,... | collective-permute-start | bytes 1327112 | tf_op jit(solution)/shard_map/ppermute | solution.py:396
  53.3 19.0 %collective-permute-start.3 = (bf16[48,4608]{1,0:T(8,128)(2,1)S(1)}, bf16[48,4608]{1,0:T(8,128)(2,1)S(1)}, u32[]{:S(2)}, u32[]{:S(2)}) collective-permute-start(bf16[48,4608]{1,0:T(8,128)(2,1)S(1)} %collective-permute-done.refs_1_), channel_id=1, source_target_pairs={{0,2},{1,3},{2,4},{3,5},{4,6},{5,7},{6,8},{7,9},{8,10},{9,11},{10,... | collective-permute-start | bytes 1327112 | tf_op jit(solution)/shard_map/ppermute | solution.py:396
  59.0 19.0 %collective-permute-start.17 = (bf16[48,4608]{1,0:T(8,128)(2,1)S(1)}, bf16[48,4608]{1,0:T(8,128)(2,1)S(1)}, u32[]{:S(2)}, u32[]{:S(2)}) collective-permute-start(bf16[48,4608]{1,0:T(8,128)(2,1)S(1)} %collective-permute-done.8.refs_4_), channel_id=1, source_target_pairs={{0,14},{1,15},{2,0},{3,1},{4,2},{5,3},{6,4},{7,5},{8,6},{9,7},{10,... | collective-permute-start | bytes 1327112 | tf_op jit(solution)/shard_map/ppermute | solution.py:396
  62.7 19.1 %collective-permute-start.16 = (bf16[48,4608]{1,0:T(8,128)(2,1)S(1)}, bf16[48,4608]{1,0:T(8,128)(2,1)S(1)}, u32[]{:S(2)}, u32[]{:S(2)}) collective-permute-start(bf16[48,4608]{1,0:T(8,128)(2,1)S(1)} %collective-permute-done.7.refs_3_), channel_id=1, source_target_pairs={{0,2},{1,3},{2,4},{3,5},{4,6},{5,7},{6,8},{7,9},{8,10},{9,11},{10,... | collective-permute-start | bytes 1327112 | tf_op jit(solution)/shard_map/ppermute | solution.py:396
  68.5 19.0 %collective-permute-start.13 = (bf16[48,4608]{1,0:T(8,128)(2,1)S(1)}, bf16[48,4608]{1,0:T(8,128)(2,1)S(1)}, u32[]{:S(2)}, u32[]{:S(2)}) collective-permute-start(bf16[48,4608]{1,0:T(8,128)(2,1)S(1)} %collective-permute-done.4.refs_4_), channel_id=1, source_target_pairs={{0,14},{1,15},{2,0},{3,1},{4,2},{5,3},{6,4},{7,5},{8,6},{9,7},{10,... | collective-permute-start | bytes 1327112 | tf_op jit(solution)/shard_map/ppermute | solution.py:396
  72.2 19.0 %collective-permute-start.12 = (bf16[48,4608]{1,0:T(8,128)(2,1)S(1)}, bf16[48,4608]{1,0:T(8,128)(2,1)S(1)}, u32[]{:S(2)}, u32[]{:S(2)}) collective-permute-start(bf16[48,4608]{1,0:T(8,128)(2,1)S(1)} %collective-permute-done.3.refs_3_), channel_id=1, source_target_pairs={{0,2},{1,3},{2,4},{3,5},{4,6},{5,7},{6,8},{7,9},{8,10},{9,11},{10,... | collective-permute-start | bytes 1327112 | tf_op jit(solution)/shard_map/ppermute | solution.py:396
  78.0 14.5 %collective-permute-start.19 = (bf16[48,2304]{1,0:T(8,128)(2,1)S(1)}, bf16[48,2304]{1,0:T(8,128)(2,1)S(1)}, u32[]{:S(2)}, u32[]{:S(2)}) collective-permute-start(bf16[48,2304]{1,0:T(8,128)(2,1)S(1)} %slice.19), channel_id=1, source_target_pairs={{0,14},{1,15},{2,0},{3,1},{4,2},{5,3},{6,4},{7,5},{8,6},{9,7},{10,... | collective-permute-start | bytes 663560 | tf_op jit(solution)/shard_map/ppermute | solution.py:396
  81.8 13.0 %collective-permute-start.18 = (bf16[48,2304]{1,0:T(8,128)(2,1)S(1)}, bf16[48,2304]{1,0:T(8,128)(2,1)S(1)}, u32[]{:S(2)}, u32[]{:S(2)}) collective-permute-start(bf16[48,2304]{1,0:T(8,128)(2,1)S(1)} %slice.18), channel_id=1, source_target_pairs={{0,2},{1,3},{2,4},{3,5},{4,6},{5,7},{6,8},{7,9},{8,10},{9,11},{10,... | collective-permute-start | bytes 663560 | tf_op jit(solution)/shard_map/ppermute | solution.py:396
  81.9 16.8 %collective-permute-start.10 = (f32[544,128]{1,0:T(8,128)S(1)}, f32[544,128]{1,0:T(8,128)S(1)}, u32[]{:S(2)}, u32[]{:S(2)}) collective-permute-start(f32[544,128]{1,0:T(8,128)S(1)} %get-tuple-element.60), channel_id=1, source_target_pairs={{0,64},{1,17},{2,66},{3,19},{4,68},{5,21},{6,70},{7,23},{8,72},{9,... | collective-permute-start | bytes 835592 | tf_op jit(solution)/shard_map/ppermute | solution.py:406
  87.5 11.2 %collective-permute-start.11 = (f32[544,128]{1,0:T(8,128)S(1)}, f32[544,128]{1,0:T(8,128)S(1)}, u32[]{:S(2)}, u32[]{:S(2)}) collective-permute-start(f32[544,128]{1,0:T(8,128)S(1)} %get-tuple-element.61), channel_id=1, source_target_pairs={{0,192},{1,49},{2,194},{3,51},{4,196},{5,53},{6,198},{7,55},{8,200... | collective-permute-start | bytes 835592 | tf_op jit(solution)/shard_map/ppermute | solution.py:406
  91.2 8.1 %collective-permute-start.9 = (f32[544,128]{1,0:T(8,128)S(1)}, f32[544,128]{1,0:T(8,128)S(1)}, u32[]{:S(2)}, u32[]{:S(2)}) collective-permute-start(f32[544,128]{1,0:T(8,128)S(1)} %get-tuple-element.59), channel_id=1, source_target_pairs={{0,128},{1,33},{2,130},{3,35},{4,132},{5,37},{6,134},{7,39},{8,136... | collective-permute-start | bytes 835592 | tf_op jit(solution)/shard_map/ppermute | solution.py:406
  92.6 6.7 %collective-permute-start.15 = (bf16[48,2304]{1,0:T(8,128)(2,1)S(1)}, bf16[48,2304]{1,0:T(8,128)(2,1)S(1)}, u32[]{:S(2)}, u32[]{:S(2)}) collective-permute-start(bf16[48,2304]{1,0:T(8,128)(2,1)S(1)} %slice.17), channel_id=1, source_target_pairs={{0,14},{1,15},{2,0},{3,1},{4,2},{5,3},{6,4},{7,5},{8,6},{9,7},{10,... | collective-permute-start | bytes 663560 | tf_op jit(solution)/shard_map/ppermute | solution.py:396
  94.8 7.1 %collective-permute-start.14 = (bf16[48,2304]{1,0:T(8,128)(2,1)S(1)}, bf16[48,2304]{1,0:T(8,128)(2,1)S(1)}, u32[]{:S(2)}, u32[]{:S(2)}) collective-permute-start(bf16[48,2304]{1,0:T(8,128)(2,1)S(1)} %slice.16), channel_id=1, source_target_pairs={{0,2},{1,3},{2,4},{3,5},{4,6},{5,7},{6,8},{7,9},{8,10},{9,11},{10,... | collective-permute-start | bytes 663560 | tf_op jit(solution)/shard_map/ppermute | solution.py:396
  106.0 7.1 %collective-permute-start.20 = (f32[352,128]{1,0:T(8,128)S(1)}, f32[352,128]{1,0:T(8,128)S(1)}, u32[]{:S(2)}, u32[]{:S(2)}) collective-permute-start(f32[352,128]{1,0:T(8,128)S(1)} %get-tuple-element.70), channel_id=1, source_target_pairs={{0,128},{1,33},{2,130},{3,35},{4,132},{5,37},{6,134},{7,39},{8,136... | collective-permute-start | bytes 540680 | tf_op jit(solution)/shard_map/ppermute | solution.py:406
  106.8 6.8 %collective-permute-start.21 = (f32[352,128]{1,0:T(8,128)S(1)}, f32[352,128]{1,0:T(8,128)S(1)}, u32[]{:S(2)}, u32[]{:S(2)}) collective-permute-start(f32[352,128]{1,0:T(8,128)S(1)} %get-tuple-element.71), channel_id=1, source_target_pairs={{0,64},{1,17},{2,66},{3,19},{4,68},{5,21},{6,70},{7,23},{8,72},{9,... | collective-permute-start | bytes 540680 | tf_op jit(solution)/shard_map/ppermute | solution.py:406
  109.4 8.5 %collective-permute-start.22 = (f32[352,128]{1,0:T(8,128)S(1)}, f32[352,128]{1,0:T(8,128)S(1)}, u32[]{:S(2)}, u32[]{:S(2)}) collective-permute-start(f32[352,128]{1,0:T(8,128)S(1)} %get-tuple-element.72), channel_id=1, source_target_pairs={{0,192},{1,49},{2,194},{3,51},{4,196},{5,53},{6,198},{7,55},{8,200... | collective-permute-start | bytes 540680 | tf_op jit(solution)/shard_map/ppermute | solution.py:406
  118.1 6.5 %collective-permute-start.23 = (f32[224,128]{1,0:T(8,128)S(1)}, f32[224,128]{1,0:T(8,128)S(1)}, u32[]{:S(2)}, u32[]{:S(2)}) collective-permute-start(f32[224,128]{1,0:T(8,128)S(1)} %get-tuple-element.74), channel_id=1, source_target_pairs={{0,32},{1,129},{2,34},{3,131},{4,36},{5,133},{6,38},{7,135},{8,40}... | collective-permute-start | bytes 344072 | tf_op jit(solution)/shard_map/ppermute | solution.py:406
  118.8 6.9 %collective-permute-start.24 = (f32[224,128]{1,0:T(8,128)S(1)}, f32[224,128]{1,0:T(8,128)S(1)}, u32[]{:S(2)}, u32[]{:S(2)}) collective-permute-start(f32[224,128]{1,0:T(8,128)S(1)} %get-tuple-element.75), channel_id=1, source_target_pairs={{0,16},{1,65},{2,18},{3,67},{4,20},{5,69},{6,22},{7,71},{8,24},{9,... | collective-permute-start | bytes 344072 | tf_op jit(solution)/shard_map/ppermute | solution.py:406
  119.1 6.6 %collective-permute-start.25 = (f32[224,128]{1,0:T(8,128)S(1)}, f32[224,128]{1,0:T(8,128)S(1)}, u32[]{:S(2)}, u32[]{:S(2)}) collective-permute-start(f32[224,128]{1,0:T(8,128)S(1)} %get-tuple-element.76), channel_id=1, source_target_pairs={{0,48},{1,193},{2,50},{3,195},{4,52},{5,197},{6,54},{7,199},{8,56}... | collective-permute-start | bytes 344072 | tf_op jit(solution)/shard_map/ppermute | solution.py:406
  125.8 7.8 %collective-permute-start.27 = (bf16[3,32,128]{2,1,0:T(8,128)(2,1)S(1)}, bf16[3,32,128]{2,1,0:T(8,128)(2,1)S(1)}, u32[]{:S(2)}, u32[]{:S(2)}) collective-permute-start(bf16[3,32,128]{2,1,0:T(8,128)(2,1)S(1)} %get-tuple-element.79), channel_id=1, source_target_pairs={{0,8},{1,9},{2,10},{3,11},{4,12},{5,13},{6,14},{7,15},{8,0},{9,1},... | collective-permute-start | bytes 73736 | tf_op jit(solution)/shard_map/ppermute | solution.py:396
  127.0 3.7 %collective-permute-start.29 = (bf16[2,32,128]{2,1,0:T(8,128)(2,1)S(1)}, bf16[2,32,128]{2,1,0:T(8,128)(2,1)S(1)}, u32[]{:S(2)}, u32[]{:S(2)}) collective-permute-start(bf16[2,32,128]{2,1,0:T(8,128)(2,1)S(1)} %get-tuple-element.80), channel_id=1, source_target_pairs={{0,14},{1,15},{2,0},{3,1},{4,2},{5,3},{6,4},{7,5},{8,6},{9,7},{10,... | collective-permute-start | bytes 49160 | tf_op jit(solution)/shard_map/ppermute | solution.py:396
  127.0 6.6 %collective-permute-start.26 = (bf16[2,32,128]{2,1,0:T(8,128)(2,1)S(1)}, bf16[2,32,128]{2,1,0:T(8,128)(2,1)S(1)}, u32[]{:S(2)}, u32[]{:S(2)}) collective-permute-start(bf16[2,32,128]{2,1,0:T(8,128)(2,1)S(1)} %get-tuple-element.78), channel_id=1, source_target_pairs={{0,2},{1,3},{2,4},{3,5},{4,6},{5,7},{6,8},{7,9},{8,10},{9,11},{10,... | collective-permute-start | bytes 49160 | tf_op jit(solution)/shard_map/ppermute | solution.py:396
  133.6 3.7 %collective-permute-start.30 = (bf16[2,32,128]{2,1,0:T(8,128)(2,1)S(1)}, bf16[2,32,128]{2,1,0:T(8,128)(2,1)S(1)}, u32[]{:S(2)}, u32[]{:S(2)}) collective-permute-start(bf16[2,32,128]{2,1,0:T(8,128)(2,1)S(1)} %gather.3), channel_id=1, source_target_pairs={{0,14},{1,15},{2,0},{3,1},{4,2},{5,3},{6,4},{7,5},{8,6},{9,7},{10,... | collective-permute-start | bytes 49160 | tf_op jit(solution)/shard_map/ppermute | solution.py:396
  133.6 5.0 %collective-permute-start.28 = (bf16[2,32,128]{2,1,0:T(8,128)(2,1)S(1)}, bf16[2,32,128]{2,1,0:T(8,128)(2,1)S(1)}, u32[]{:S(2)}, u32[]{:S(2)}) collective-permute-start(bf16[2,32,128]{2,1,0:T(8,128)(2,1)S(1)} %gather.2), channel_id=1, source_target_pairs={{0,2},{1,3},{2,4},{3,5},{4,6},{5,7},{6,8},{7,9},{8,10},{9,11},{10,... | collective-permute-start | bytes 49160 | tf_op jit(solution)/shard_map/ppermute | solution.py:396
